TPU v7x, 256 devices: a whole 4x4x8 slice. The times are simulated.
256 devices in a mesh: section: 2 (over z_lo), tok: 4 (over z_hi), vocab: 32 (over x, y, core).
Axes of the slice: x: 4, y: 4, z: 8 (z_hi: 4, z_lo: 2; z = z_hi * 2 + z_lo), core: 2. Of those that a mesh axis runs over, the one named last changes fastest.
Arguments:
- hidden: bfloat16 [2, 256, 8192], P('section', 'tok', 'vocab'), may hold values from -40 to 40
- head: bfloat16 [2, 8192, 64128], P('section', None, ('tok', 'vocab')), may hold values from -1.0535376 to 1.0535376
- token_ids: int32 [256], replicated, may hold values from 0 to 64127
- loss_mask: int32 [256], replicated, may hold values 0 or 1
Outputs:
- head_grad: bfloat16 [8192, 64128], P('section', ('tok', 'vocab'))
- hidden_grad: bfloat16 [256, 8192], P('tok', ('section', 'vocab'))
All inputs are finite; a program needn't handle non-finite values.
Results may differ from a plain program's by a relative error of at most 0.018.
Values may be sent and summed in bfloat16 or wider, within the bound.
No kernel may reach another device: no remote copies, remote signals or barrier semaphores. Data moves between devices by JAX's collectives and lax.ppermute only.
A program may use at most 128 MiB of HBM per device.

v0:
```python
import functools
import jax
import jax.numpy as jnp
from jax import lax
from jax.experimental import pallas as pl
from jax.experimental.pallas import tpu as pltpu
from jax.sharding import PartitionSpec as P

AXES = ("section", "tok", "vocab")
SIZES = {"s": 2, "t": 4, "x": 4, "y": 4, "c": 2}
MIB = 1024 * 1024


def route(shift_of):
    names = list(SIZES)
    pairs = []
    for device in range(256):
        place, rest = {}, device
        for name in reversed(names):
            rest, place[name] = divmod(rest, SIZES[name])
        shift = shift_of(place)
        target = 0
        for name in names:
            target = target * SIZES[name] + (place[name] + shift.get(name, 0)) % SIZES[name]
        pairs.append((device, target))
    return pairs


def send(block, **shift):
    return lax.ppermute(block, AXES, route(lambda place: shift))


def send_by_core(block, even, odd):
    return lax.ppermute(block, AXES, route(lambda place: odd if place["c"] else even))


def send_both_ways(block):
    def shift_of(place):
        return {"s": 1, "t": (1 if place["s"] else 3) if place["c"] else 0}

    return lax.ppermute(block, AXES, route(shift_of))


def params(mib):
    return pltpu.CompilerParams(vmem_limit_bytes=mib * MIB)


BRIEF = pl.CostEstimate(flops=0, bytes_accessed=0, transcendentals=0)
VMEM = pl.BlockSpec(memory_space=pltpu.VMEM)
SMEM = pl.BlockSpec(memory_space=pltpu.SMEM)


def piece_columns(place_ref, core, d, e):
    at_x = (place_ref[2] + jnp.where(core == 0, d, e)) % 4
    at_y = (place_ref[3] + jnp.where(core == 0, e, d)) % 4
    return pl.ds(pl.multiple_of((core * 16 + at_x * 4 + at_y) * 256, 256), 256)


def stage_kernel(place_ref, head_ref, out_ref, *refs):
    gives, arrived = refs[:8], refs[8]
    copy = pltpu.make_async_copy(head_ref, out_ref, arrived)
    copy.start()
    for d in range(4):
        for e in range(4):
            columns = piece_columns(place_ref, 1 - place_ref[4], d, e)
            gives[2 * d + e // 2][:, e % 2 * 256 : e % 2 * 256 + 256] = head_ref[:, columns]
    copy.wait()


def stage(place, head_t):
    width, _ = head_t.shape
    return pl.pallas_call(
        stage_kernel,
        out_shape=[jax.ShapeDtypeStruct(head_t.shape, head_t.dtype)]
        + [jax.ShapeDtypeStruct((width, 512), head_t.dtype)] * 8,
        in_specs=[SMEM, VMEM],
        out_specs=[VMEM] * 9,
        scratch_shapes=[pltpu.SemaphoreType.DMA],
        compiler_params=params(22),
    )(place, head_t)


def first_half_kernel(place_ref, *refs):
    own, out_ref = refs[:4], refs[4]
    tok, x, y, c = place_ref[1], place_ref[2], place_ref[3], place_ref[4]
    _, _, rows, chunk = own[0].shape

    def lay(x_at, y_at, piece):
        columns = pl.ds(pl.multiple_of(y_at * chunk, chunk), chunk)
        for dt in range(4):
            at = pl.ds(pl.multiple_of((tok + 4 - dt) % 4 * rows, rows), rows)
            out_ref[x_at, at, columns] = piece(dt)

    for x_at in range(2):
        dx = (x + 4 - x_at) % 4

        @pl.when(c == 0)
        def _():
            for dy in range(4):
                lay(x_at, (y + 4 - dy) % 4, lambda dt: own[dy][dx, dt])

        for step in range(4):
            @pl.when(jnp.logical_and(c == 1, dx == step))
            def _():
                for dy in range(4):
                    lay(x_at, (y + 4 - dy) % 4, lambda dt: own[step][dy, dt])


def first_half(place, own):
    _, _, rows, chunk = own[0].shape
    return pl.pallas_call(
        first_half_kernel,
        out_shape=jax.ShapeDtypeStruct((2, 4 * rows, 4 * chunk), own[0].dtype),
        in_specs=[SMEM] + [VMEM] * 4,
        out_specs=VMEM,
        compiler_params=params(5),
        cost_estimate=BRIEF,
    )(place, *own)


def lay_out(place_ref, core, blocks, hidden_ref):
    tok, x, y = place_ref[1], place_ref[2], place_ref[3]
    _, _, rows, chunk = blocks[0].shape
    for late in range(4):
        for early in range(4):
            at_x = (x + 4 - jnp.where(core == 0, early, late)) % 4
            at_y = (y + 4 - jnp.where(core == 0, late, early)) % 4
            columns = pl.ds(pl.multiple_of(at_y * chunk, chunk), chunk)
            for dt in range(4):
                at = pl.ds(pl.multiple_of((tok + 4 - dt) % 4 * rows, rows), rows)
                hidden_ref[at_x, at, columns] = blocks[late][early, dt]


def add_products(core, head_ref, hidden_ref, acc_ref):
    chunk = hidden_ref.shape[2] // 4

    @pl.loop(0, 4)
    def _(x):
        total = acc_ref[...]
        for y in range(4):
            columns = pl.ds(pl.multiple_of(((x * 4 + y) * 2 + core) * chunk, chunk), chunk)
            total += lax.dot_general(
                head_ref[:, columns],
                hidden_ref[x, :, y * chunk : y * chunk + chunk],
                (((1,), (1,)), ((), ())),
                preferred_element_type=jnp.float32,
            )
        acc_ref[...] = total


def own_logits_kernel(place_ref, head_ref, *refs):
    own, (hidden_ref, acc_ref) = refs[:4], refs[4:]
    lay_out(place_ref, place_ref[4], own, hidden_ref)
    acc_ref[...] = jnp.zeros_like(acc_ref)
    add_products(place_ref[4], head_ref, hidden_ref, acc_ref)


def own_logits(place, head_t, own):
    width, _ = head_t.shape
    _, _, rows, chunk = own[0].shape
    toks = 4 * rows
    return pl.pallas_call(
        own_logits_kernel,
        out_shape=[
            jax.ShapeDtypeStruct((4, toks, 4 * chunk), jnp.bfloat16),
            jax.ShapeDtypeStruct((width, toks), jnp.float32),
        ],
        in_specs=[SMEM] + [VMEM] * 5,
        out_specs=[VMEM] * 2,
        compiler_params=params(16),
    )(place, head_t, *own)


def logits_kernel(place_ref, head_ref, *refs):
    other, part_ref = refs[:4], refs[4]
    hidden_ref, scaled_ref, short_ref, stats_ref, acc_ref = refs[5:]
    lay_out(place_ref, 1 - place_ref[4], other, hidden_ref)
    acc_ref[...] = part_ref[...]
    add_products(1 - place_ref[4], head_ref, hidden_ref, acc_ref)
    logits = acc_ref[...]
    peak = jnp.max(logits, axis=0, keepdims=True)
    shifted = logits - peak
    scaled = jnp.exp(shifted)
    scaled_ref[...] = scaled
    short_ref[...] = scaled.astype(jnp.bfloat16)
    stats_ref[0:1] = peak
    stats_ref[1:2] = jnp.sum(scaled, axis=0, keepdims=True)
    stats_ref[2:3] = jnp.sum(scaled * shifted, axis=0, keepdims=True)
    stats_ref[3:8] = jnp.zeros((5, peak.shape[1]), jnp.float32)


def logits_parts(place, head_t, other, part):
    width, toks = part.shape
    _, _, rows, chunk = other[0].shape
    return pl.pallas_call(
        logits_kernel,
        out_shape=[
            jax.ShapeDtypeStruct((4, toks, 4 * chunk), jnp.bfloat16),
            jax.ShapeDtypeStruct((width, toks), jnp.float32),
            jax.ShapeDtypeStruct((width, toks), jnp.bfloat16),
            jax.ShapeDtypeStruct((8, toks), jnp.float32),
        ],
        in_specs=[SMEM] + [VMEM] * 6,
        out_specs=[VMEM] * 4,
        scratch_shapes=[pltpu.VMEM((width, toks), jnp.float32)],
        compiler_params=params(17),
        cost_estimate=BRIEF,
    )(place, head_t, *other, part)


def merge_kernel(*refs):
    *ins, out_ref = refs
    peak = ins[0][0:1]
    for ref in ins[1:]:
        peak = jnp.maximum(peak, ref[0:1])
    total = jnp.zeros_like(peak)
    moment = jnp.zeros_like(peak)
    for ref in ins:
        drop = ref[0:1] - peak
        factor = jnp.exp(drop)
        total += factor * ref[1:2]
        moment += factor * (ref[2:3] + drop * ref[1:2])
    out_ref[0:1] = peak
    out_ref[1:2] = total
    out_ref[2:3] = moment
    out_ref[3:8] = jnp.zeros((5, peak.shape[1]), jnp.float32)


def merge(*stats):
    return pl.pallas_call(
        merge_kernel,
        out_shape=jax.ShapeDtypeStruct(stats[0].shape, jnp.float32),
        in_specs=[VMEM] * len(stats),
        out_specs=VMEM,
        compiler_params=params(1),
        cost_estimate=BRIEF,
    )(*stats)


def scale_kernel(local_ref, *refs):
    *ins, out_ref = refs
    peak = ins[0][0:1]
    for ref in ins[1:]:
        peak = jnp.maximum(peak, ref[0:1])
    total = jnp.zeros_like(peak)
    moment = jnp.zeros_like(peak)
    for ref in ins:
        drop = ref[0:1] - peak
        factor = jnp.exp(drop)
        total += factor * ref[1:2]
        moment += factor * (ref[2:3] + drop * ref[1:2])
    out_ref[0:1] = jnp.exp(local_ref[0:1] - peak) / total
    out_ref[1:2] = jnp.log(total) - moment / total
    out_ref[2:8] = jnp.zeros((6, peak.shape[1]), jnp.float32)


def local_scale(local, *stats):
    return pl.pallas_call(
        scale_kernel,
        out_shape=jax.ShapeDtypeStruct(local.shape, jnp.float32),
        in_specs=[VMEM] * (1 + len(stats)),
        out_specs=VMEM,
        compiler_params=params(1),
        cost_estimate=BRIEF,
    )(local, *stats)


def grad_kernel(place_ref, own_ref, other_ref, own_stats, other_stats, ids_ref, mask_ref, grad_ref, turned_ref):
    teacher = place_ref[0] == 0
    mask = mask_ref[...].astype(jnp.float32)
    entropy = jnp.where(teacher, own_stats[1:2], other_stats[1:2])
    by_own = jnp.where(teacher, -entropy, entropy + 1.0) * own_stats[0:1] * mask
    by_other = jnp.where(teacher, entropy + 1.0, -entropy) * other_stats[0:1] * mask
    width = own_ref.shape[0]
    first = ((place_ref[1] * 4 + place_ref[2]) * 8 + place_ref[3] * 2 + place_ref[4]) * width
    entries = lax.broadcasted_iota(jnp.int32, own_ref.shape, 0) + first
    onehot = jnp.where(entries == ids_ref[...], mask, 0.0)
    grad = by_own * own_ref[...] + by_other * other_ref[...].astype(jnp.float32) - onehot
    grad_ref[...] = grad.astype(jnp.bfloat16)
    turned_ref[...] = grad.T.astype(jnp.bfloat16)


def logits_grad(place, own, other, own_stats, other_stats, ids, mask):
    width, toks = own.shape
    return pl.pallas_call(
        grad_kernel,
        out_shape=[
            jax.ShapeDtypeStruct((width, toks), jnp.bfloat16),
            jax.ShapeDtypeStruct((toks, width), jnp.bfloat16),
        ],
        in_specs=[SMEM] + [VMEM] * 6,
        out_specs=[VMEM, VMEM],
        compiler_params=params(5),
        cost_estimate=BRIEF,
    )(place, own, other, own_stats, other_stats, ids, mask)


def own_products_kernel(d, place_ref, turned_ref, head_ref, out_ref):
    for e in range(4):
        out_ref[e] = jnp.dot(
            turned_ref[...],
            head_ref[:, piece_columns(place_ref, place_ref[4], d, e)],
            preferred_element_type=jnp.float32,
        )


def own_products(place, turned, head_t, d):
    return pl.pallas_call(
        functools.partial(own_products_kernel, d),
        out_shape=jax.ShapeDtypeStruct((4, turned.shape[0], 256), jnp.float32),
        in_specs=[SMEM, VMEM, VMEM],
        out_specs=VMEM,
        compiler_params=params(11),
        cost_estimate=BRIEF,
    )(place, turned, head_t)


def products_kernel(d, place_ref, turned_ref, head_ref, twin_ref, *refs):
    halves, parts, out_ref = refs[:2], refs[2:-1], refs[-1]
    for e in range(4):
        total = jnp.dot(
            twin_ref[...],
            halves[e // 2][:, e % 2 * 256 : e % 2 * 256 + 256],
            preferred_element_type=jnp.float32,
        )
        if parts:
            total += parts[0][e]
        else:
            total += jnp.dot(
                turned_ref[...],
                head_ref[:, piece_columns(place_ref, place_ref[4], d, e)],
                preferred_element_type=jnp.float32,
            )
        out_ref[e] = total.astype(jnp.bfloat16)


def products(place, turned, head_t, twin, halves, d, *parts):
    toks = turned.shape[0]
    return pl.pallas_call(
        functools.partial(products_kernel, d),
        out_shape=jax.ShapeDtypeStruct((4, toks, 256), jnp.bfloat16),
        in_specs=[SMEM] + [VMEM] * (5 + len(parts)),
        out_specs=VMEM,
        compiler_params=params(13),
        cost_estimate=BRIEF,
    )(place, turned, head_t, twin, *halves, *parts)


def add_split_kernel(*refs):
    ins, outs = refs[:4], refs[4:]
    for d, out_ref in enumerate(outs):
        total = ins[0][d].astype(jnp.float32)
        for ref in ins[1:]:
            total += ref[d].astype(jnp.float32)
        out_ref[...] = total.astype(out_ref.dtype)


def add_split(*blocks):
    return pl.pallas_call(
        add_split_kernel,
        out_shape=[jax.ShapeDtypeStruct(blocks[0].shape[1:], blocks[0].dtype)] * 4,
        in_specs=[VMEM] * 4,
        out_specs=[VMEM] * 4,
        compiler_params=params(6),
        cost_estimate=BRIEF,
    )(*blocks)


def add_rows_kernel(place_ref, *refs):
    ins, outs, sum_ref = refs[:4], refs[4:8], refs[8]
    tok = place_ref[1]
    total = ins[0][...].astype(jnp.float32)
    for ref in ins[1:]:
        total += ref[...].astype(jnp.float32)
    sum_ref[...] = total.astype(sum_ref.dtype)
    block = outs[0].shape[0]
    for d, out_ref in enumerate(outs):
        out_ref[...] = sum_ref[pl.ds(pl.multiple_of((tok + d) % 4 * block, block), block), :]


def add_rows(place, blocks):
    toks, wide = blocks[0].shape
    return pl.pallas_call(
        add_rows_kernel,
        out_shape=[jax.ShapeDtypeStruct((toks // 4, wide), jnp.bfloat16)] * 4,
        in_specs=[SMEM] + [VMEM] * 4,
        out_specs=[VMEM] * 4,
        scratch_shapes=[pltpu.VMEM((toks, wide), jnp.bfloat16)],
        compiler_params=params(2),
        cost_estimate=BRIEF,
    )(place, *blocks)


def add_toks_kernel(place_ref, own_ref, *refs):
    ins, (keep_ref, give_ref) = refs[:4], refs[4:]
    even = place_ref[4] == 0
    first = jnp.where(even, ins[0][...].astype(jnp.float32), own_ref[...].astype(jnp.float32))
    total = first
    for ref in ins[1:]:
        total += ref[...].astype(jnp.float32)
    left, right = total[:, :128], total[:, 128:]
    keep_ref[...] = jnp.where(even, left, right).astype(keep_ref.dtype)
    give_ref[...] = jnp.where(even, right, left).astype(give_ref.dtype)


def add_toks(place, own, *received):
    rows, wide = own.shape
    return pl.pallas_call(
        add_toks_kernel,
        out_shape=[jax.ShapeDtypeStruct((rows, wide // 2), jnp.bfloat16)] * 2,
        in_specs=[SMEM] + [VMEM] * 5,
        out_specs=[VMEM] * 2,
        compiler_params=params(1),
        cost_estimate=BRIEF,
    )(place, own, *received)


def choose_kernel(place_ref, keep_ref, got_ref, out_ref):
    mine = place_ref[0] == place_ref[4]
    keep, got = keep_ref[...].astype(jnp.float32), got_ref[...].astype(jnp.float32)
    out_ref[...] = jnp.where(mine, keep, got).astype(out_ref.dtype)


def choose(place, keep, got):
    return pl.pallas_call(
        choose_kernel,
        out_shape=jax.ShapeDtypeStruct(keep.shape, keep.dtype),
        in_specs=[SMEM, VMEM, VMEM],
        out_specs=VMEM,
        compiler_params=params(1),
        cost_estimate=BRIEF,
    )(place, keep, got)


def head_grad_kernel(place_ref, grad_ref, own_ref, other_ref, sent_ref, twin_ref, out_ref):
    teacher = place_ref[0] == 0
    core = place_ref[4]

    def write(mine, others):
        for y in range(2):
            for ref, part in ((mine, core), (others, 1 - core)):
                columns = pl.ds(pl.multiple_of((y * 2 + part) * 256, 256), 256)
                out_ref[:, columns] = jnp.dot(
                    grad_ref[...], ref[0, :, 256 * y : 256 * y + 256], preferred_element_type=jnp.float32
                ).astype(jnp.bfloat16)

    @pl.when(teacher)
    def _():
        write(sent_ref, twin_ref)

    @pl.when(jnp.logical_not(teacher))
    def _():
        write(own_ref, other_ref)


def head_grad_half(place, grad, own, other, sent, twin):
    width, toks = grad.shape
    block = own.shape[2]
    second = pl.BlockSpec((1, toks, block // 2), lambda step, place: (2 + step // 2, 0, step % 2))
    first = pl.BlockSpec((1, toks, block // 2), lambda step, place: (step // 2, 0, step % 2))
    return pl.pallas_call(
        head_grad_kernel,
        grid_spec=pltpu.PrefetchScalarGridSpec(
            num_scalar_prefetch=1,
            grid=(4,),
            in_specs=[
                pl.BlockSpec((width, toks), lambda step, place: (0, 0)),
                second,
                second,
                first,
                first,
            ],
            out_specs=pl.BlockSpec((width, block), lambda step, place: (0, step)),
        ),
        out_shape=jax.ShapeDtypeStruct((width, 4 * block), jnp.bfloat16),
        compiler_params=params(8),
        cost_estimate=BRIEF,
    )(place, grad, own, other, sent, twin)


def spread(stats, name):
    far = send(stats, **{name: 2})
    near = send_by_core(stats, {name: 1}, {name: 3})
    return [stats, far, near, send(near, c=1)]


def on_device(hidden, head, token_ids, loss_mask):
    section, tok, vocab = (lax.axis_index(name) for name in AXES)
    place = jnp.stack([section, tok, vocab >> 3, (vocab >> 1) & 3, vocab & 1]).astype(jnp.int32)
    states = hidden[0]

    with jax.named_scope("gather_tok"):
        blocks = [states] + [send(states, t=d) for d in (1, 2, 3)]
    with jax.named_scope("stage"):
        head_t, *halves = stage(place, head[0].T)
        head_t, *blocks = lax.optimization_barrier((head_t, *blocks))
        halves = [send(half, c=1) for half in halves]
    with jax.named_scope("gather_tok"):
        block = jnp.stack(blocks)
    with jax.named_scope("gather_first"):
        blocks = [block] + [send_by_core(block, {"x": d}, {"y": d}) for d in (1, 2, 3)]
    with jax.named_scope("gather_first"):
        block = jnp.stack(blocks)
    with jax.named_scope("gather_second"):
        own = [block] + [send_by_core(block, {"y": d}, {"x": d}) for d in (1, 2, 3)]
    own[1], halves = lax.optimization_barrier((own[1], halves))
    with jax.named_scope("gather_cores"):
        other = [send(block, c=1) for block in own[:3]]
        own[3], *other = lax.optimization_barrier((own[3], *other))
        other.append(send(own[3], c=1))
    with jax.named_scope("student_hidden"):
        sent = send_both_ways(first_half(place, own))
    with jax.named_scope("own_logits"):
        hidden_own, part = own_logits(place, head_t, own)
    with jax.named_scope("logits"):
        hidden_other, scaled, short, local = logits_parts(place, head_t, other, part)

    with jax.named_scope("stats"):
        stats = merge(local, send(local, c=1))
        stats, short = lax.optimization_barrier((stats, short))
    with jax.named_scope("exchange_scaled"):
        other_short = send(short, s=1)
    with jax.named_scope("stats"):
        stats = merge(*spread(stats, "x"))
        stats, sent = lax.optimization_barrier((stats, sent))
    with jax.named_scope("student_hidden"):
        twin = send(sent, c=1)
    with jax.named_scope("stats"):
        stats = merge(*spread(stats, "y"))
        own_stats = local_scale(local, *spread(stats, "t"))
        other_stats = send(own_stats, s=1)

    with jax.named_scope("logits_grad"):
        grad, turned = logits_grad(
            place, scaled, other_short, own_stats, other_stats, token_ids[None], loss_mask[None]
        )
    turned, twin = lax.optimization_barrier((turned, twin))
    sums, firsts = [], []
    with jax.named_scope("hidden_grad"):
        turned_twin = send(turned, c=1)
        part = own_products(place, turned, head_t, 1)
        part, turned_twin = lax.optimization_barrier((part, turned_twin))
        for d in (1, 2, 3, 0):
            parts = (part,) if d == 1 else ()
            if d == 0:
                turned, firsts[0] = lax.optimization_barrier((turned, firsts[0]))
            sums.append(products(place, turned, head_t, turned_twin, halves[2 * d : 2 * d + 2], d, *parts))
            turned, sums[-1] = lax.optimization_barrier((turned, sums[-1]))
            if d > 0:
                firsts.append(send_by_core(sums[-1], {"x": d}, {"y": d}))
    with jax.named_scope("head_grad"):
        head_out = head_grad_half(place, grad, hidden_own, hidden_other, sent, twin)
        firsts[1], head_out = lax.optimization_barrier((firsts[1], head_out))
    with jax.named_scope("reduce_second"):
        parts = add_split(sums[3], *firsts)
        seconds = [send_by_core(parts[d], {"y": d}, {"x": d}) for d in (1, 2, 3)]
    with jax.named_scope("reduce_tok"):
        rows = add_rows(place, [parts[0]] + seconds)
        received = [send(rows[0], s=1)]
        received += [send_by_core(rows[d], {"s": 1, "t": d}, {"t": d}) for d in (1, 2, 3)]
        keep, give = add_toks(place, rows[0], *received)
    with jax.named_scope("hidden_out"):
        hidden_out = choose(place, keep, send(give, c=1))
    return head_out.T, hidden_out


def solution(mesh):
    in_specs = (P("section", "tok", "vocab"), P("section", None, ("tok", "vocab")), P(), P())
    out_specs = (P("section", ("tok", "vocab")), P("tok", ("section", "vocab")))
    return jax.shard_map(
        on_device, mesh=mesh, in_specs=in_specs, out_specs=out_specs, check_vma=False
    )
```

profile of v0, /device:TPU:1, one launch (start us, length us, event | category | flops | bytes accessed | tf_op | source)
XLA Modules:
  0.0 130.4 jit_solution(3950900961643754215)
XLA Ops:
  0.6 3.9 %collective-permute-start = (bf16[64,256]{1,0:T(8,128)(2,1)}, bf16[64,256]{1,0:T(8,128)(2,1)S(1)}, u32[]{:S(2)}, u32[]{:S(2)}) collective-permute-start(bf16[64,256]{1,0:T(8,128)(2,1)} %bitcast.28), channel_id=1, source_target_pairs={{0,32},{1,33},{2,34},{3,35},{4,36},{5,37},{6,38},{7,39},{8,40},{9,... | collective-permute-start | bytes 98312 | tf_op jit(solution)/shard_map/gather_tok/ppermute | solution.py:30
  4.5 5.1 %collective-permute-start.1 = (bf16[64,256]{1,0:T(8,128)(2,1)}, bf16[64,256]{1,0:T(8,128)(2,1)S(1)}, u32[]{:S(2)}, u32[]{:S(2)}) collective-permute-start(bf16[64,256]{1,0:T(8,128)(2,1)} %bitcast.29), channel_id=1, source_target_pairs={{0,64},{1,65},{2,66},{3,67},{4,68},{5,69},{6,70},{7,71},{8,72},{9,... | collective-permute-start | bytes 98312 | tf_op jit(solution)/shard_map/gather_tok/ppermute | solution.py:30
  9.6 2.4 %collective-permute-start.2 = (bf16[64,256]{1,0:T(8,128)(2,1)}, bf16[64,256]{1,0:T(8,128)(2,1)S(1)}, u32[]{:S(2)}, u32[]{:S(2)}) collective-permute-start(bf16[64,256]{1,0:T(8,128)(2,1)} %bitcast.30), channel_id=1, source_target_pairs={{0,96},{1,97},{2,98},{3,99},{4,100},{5,101},{6,102},{7,103},{8,104... | collective-permute-start | bytes 98312 | tf_op jit(solution)/shard_map/gather_tok/ppermute | solution.py:30
  12.1 3.3 %copy-done = bf16[1,8192,501]{1,2,0:T(8,128)(2,1)S(1)} copy-done((bf16[1,8192,501]{1,2,0:T(8,128)(2,1)S(1)}, bf16[1,8192,501]{1,2,0:T(8,128)(2,1)}, u32[]{:S(2)}) %copy-start) | copy-done | bytes 8208408
  18.8 2.6 %collective-permute-start.4 = (bf16[4,64,256]{2,1,0:T(8,128)(2,1)S(1)}, bf16[4,64,256]{2,1,0:T(8,128)(2,1)S(1)}, u32[]{:S(2)}, u32[]{:S(2)}) collective-permute-start(bf16[4,64,256]{2,1,0:T(8,128)(2,1)S(1)} %get-tuple-element.131), channel_id=1, source_target_pairs={{0,16},{1,5},{2,18},{3,7},{4,20},{5,1},{6,22},{7,3},{8,24},{9,13},... | collective-permute-start | bytes 393224 | tf_op jit(solution)/shard_map/gather_first/ppermute | solution.py:34
  22.5 2.2 %collective-permute-start.10 = (bf16[501,512]{1,0:T(8,128)(2,1)S(1)}, bf16[501,512]{1,0:T(8,128)(2,1)S(1)}, u32[]{:S(2)}, u32[]{:S(2)}) collective-permute-start(bf16[501,512]{1,0:T(8,128)(2,1)S(1)} %get-tuple-element.73), channel_id=1, source_target_pairs={{0,1},{1,0},{2,3},{3,2},{4,5},{5,4},{6,7},{7,6},{8,9},{9,8},{10,11... | collective-permute-start | bytes 1539080 | tf_op jit(solution)/shard_map/stage/ppermute | solution.py:30
  25.2 2.4 %collective-permute-start.13 = (bf16[501,512]{1,0:T(8,128)(2,1)S(1)}, bf16[501,512]{1,0:T(8,128)(2,1)S(1)}, u32[]{:S(2)}, u32[]{:S(2)}) collective-permute-start(bf16[501,512]{1,0:T(8,128)(2,1)S(1)} %get-tuple-element.76), channel_id=1, source_target_pairs={{0,1},{1,0},{2,3},{3,2},{4,5},{5,4},{6,7},{7,6},{8,9},{9,8},{10,11... | collective-permute-start | bytes 1539080 | tf_op jit(solution)/shard_map/stage/ppermute | solution.py:30
  29.4 2.6 %collective-permute-start.18 = (bf16[4,4,64,256]{3,2,1,0:T(8,128)(2,1)S(1)}, bf16[4,4,64,256]{3,2,1,0:T(8,128)(2,1)S(1)}, u32[]{:S(2)}, u32[]{:S(2)}) collective-permute-start(bf16[4,4,64,256]{3,2,1,0:T(8,128)(2,1)S(1)} %pad_maximum_fusion.refs_0_), channel_id=1, source_target_pairs={{0,4},{1,17},{2,6},{3,19},{4,0},{5,21},{6,2},{7,23},{8,12},{9,25},... | collective-permute-start | bytes 1572872 | tf_op jit(solution)/shard_map/gather_second/ppermute | solution.py:34
  34.4 2.4 %collective-permute-start.6 = (bf16[4,4,64,256]{3,2,1,0:T(8,128)(2,1)S(1)}, bf16[4,4,64,256]{3,2,1,0:T(8,128)(2,1)S(1)}, u32[]{:S(2)}, u32[]{:S(2)}) collective-permute-start(bf16[4,4,64,256]{3,2,1,0:T(8,128)(2,1)S(1)} %pad_maximum_fusion.refs_0_), channel_id=1, source_target_pairs={{0,6},{1,25},{2,0},{3,27},{4,2},{5,29},{6,4},{7,31},{8,14},{9,1},{... | collective-permute-start | bytes 1572872 | tf_op jit(solution)/shard_map/gather_second/ppermute | solution.py:34
  38.8 5.6 %collective-permute-done.18.refs_2_ = bf16[4,4,64,256]{3,2,1,0:T(8,128)(2,1)S(1)} collective-permute-done((bf16[4,4,64,256]{3,2,1,0:T(8,128)(2,1)S(1)}, bf16[4,4,64,256]{3,2,1,0:T(8,128)(2,1)S(1)}, u32[]{:S(2)}, u32[]{:S(2)}) %collective-permute-start.18) | collective-permute-done | bytes 524320 | tf_op jit(solution)/shard_map/gather_second/ppermute | solution.py:34
  49.4 2.9 %own_logits.1 = (bf16[4,256,1024]{2,1,0:T(8,128)(2,1)S(1)}, f32[501,256]{1,0:T(8,128)S(1)}) custom-call(s32[5]{0:T(128)S(1)} %stack.53.place_ref, bf16[501,8192]{1,0:T(8,128)(2,1)S(1)} %get-tuple-element.67.head_ref, bf16[4,4,64,256]{3,2,1,0:T(8,128)(2,1)S(1)} %pad_maximum_fusion.refs_0_, bf16[4,4,64,256]{3,2,1,0:T(8,128)(2,1)S(1)} %collective-permute-done.8.refs_1_, ...), custom_call_target="tpu_custom_call" | custom-call | tf_op jit(solution)/shard_map/own_logits/pallas_call | solution.py:162
  52.4 3.2 %logits.1 = (bf16[4,256,1024]{2,1,0:T(8,128)(2,1)S(1)}, f32[501,256]{1,0:T(8,128)S(1)}, bf16[501,256]{1,0:T(8,128)(2,1)S(1)}, f32[8,256]{1,0:T(8,128)S(1)}) custom-call(s32[5]{0:T(128)S(1)} %stack.53.place_ref, bf16[501,8192]{1,0:T(8,128)(2,1)S(1)} %get-tuple-element.67.head_ref, bf16[4,4,64,256]{3,2,1,0:T(8,128)(2,1)S(1)} %collective-permute-done.7.refs_0_, ...), custom_call_target="tpu_custom_call" | custom-call | tf_op jit(solution)/shard_map/logits/pallas_call | solution.py:195
  56.8 2.4 %collective-permute-start.24 = (f32[8,256]{1,0:T(8,128)S(1)}, f32[8,256]{1,0:T(8,128)S(1)}, u32[]{:S(2)}, u32[]{:S(2)}) collective-permute-start(f32[8,256]{1,0:T(8,128)S(1)} %stats.4.refs_0_), channel_id=1, source_target_pairs={{0,8},{1,25},{2,10},{3,27},{4,12},{5,29},{6,14},{7,31},{8,16},{9,1... | collective-permute-start | bytes 24584 | tf_op jit(solution)/shard_map/stats/ppermute | solution.py:34
  67.1 2.6 %collective-permute-start.29 = (f32[8,256]{1,0:T(8,128)S(1)}, f32[8,256]{1,0:T(8,128)S(1)}, u32[]{:S(2)}, u32[]{:S(2)}) collective-permute-start(f32[8,256]{1,0:T(8,128)S(1)} %collective-permute-done.28.refs_2_), channel_id=1, source_target_pairs={{0,1},{1,0},{2,3},{3,2},{4,5},{5,4},{6,7},{7,6},{8,9},{9,8},{10,11... | collective-permute-start | bytes 24584 | tf_op jit(solution)/shard_map/stats/ppermute | solution.py:30
  74.1 2.7 %collective-permute-start.32 = (f32[8,256]{1,0:T(8,128)S(1)}, f32[8,256]{1,0:T(8,128)S(1)}, u32[]{:S(2)}, u32[]{:S(2)}) collective-permute-start(f32[8,256]{1,0:T(8,128)S(1)} %collective-permute-done.31.refs_2_), channel_id=1, source_target_pairs={{0,1},{1,0},{2,3},{3,2},{4,5},{5,4},{6,7},{7,6},{8,9},{9,8},{10,11... | collective-permute-start | bytes 24584 | tf_op jit(solution)/shard_map/stats/ppermute | solution.py:30
  76.8 2.2 %collective-permute-done.30.refs_1_ = f32[8,256]{1,0:T(8,128)S(1)} collective-permute-done((f32[8,256]{1,0:T(8,128)S(1)}, f32[8,256]{1,0:T(8,128)S(1)}, u32[]{:S(2)}, u32[]{:S(2)}) %collective-permute-start.30) | collective-permute-done | bytes 8224 | tf_op jit(solution)/shard_map/stats/ppermute | solution.py:30
  79.3 2.5 %collective-permute-done.33.other_stats = f32[8,256]{1,0:T(8,128)S(1)} collective-permute-done((f32[8,256]{1,0:T(8,128)S(1)}, f32[8,256]{1,0:T(8,128)S(1)}, u32[]{:S(2)}, u32[]{:S(2)}) %collective-permute-start.33) | collective-permute-done | bytes 8224 | tf_op jit(solution)/shard_map/stats/ppermute | solution.py:30
  88.9 3.0 %collective-permute-start.36 = (bf16[4,256,256]{2,1,0:T(8,128)(2,1)S(1)}, bf16[4,256,256]{2,1,0:T(8,128)(2,1)S(1)}, u32[]{:S(2)}, u32[]{:S(2)}) collective-permute-start(bf16[4,256,256]{2,1,0:T(8,128)(2,1)S(1)} %hidden_grad.7), channel_id=1, source_target_pairs={{0,16},{1,5},{2,18},{3,7},{4,20},{5,1},{6,22},{7,3},{8,24},{9,13},... | collective-permute-start | bytes 1572872 | tf_op jit(solution)/shard_map/hidden_grad/ppermute | solution.py:34
  92.3 4.4 %head_grad.1 = bf16[501,4096]{1,0:T(8,128)(2,1)} custom-call(s32[5]{0:T(128)S(1)} %stack.53.place_ref, bf16[501,256]{1,0:T(8,128)(2,1)S(1)} %get-tuple-element.103.grad_ref, bf16[4,256,1024]{2,1,0:T(8,128)(2,1)S(1)} %get-tuple-element.104.own_ref, bf16[4,256,1024]{2,1,0:T(8,128)(2,1)S(1)} %get-tuple-element.105.other_ref, ...), custom_call_target="tpu_custom_call" | custom-call | tf_op jit(solution)/shard_map/head_grad/pallas_call | solution.py:461
  98.0 3.7 %collective-permute-done.36.refs_2_ = bf16[4,256,256]{2,1,0:T(8,128)(2,1)S(1)} collective-permute-done((bf16[4,256,256]{2,1,0:T(8,128)(2,1)S(1)}, bf16[4,256,256]{2,1,0:T(8,128)(2,1)S(1)}, u32[]{:S(2)}, u32[]{:S(2)}) %collective-permute-start.36) | collective-permute-done | bytes 524320 | tf_op jit(solution)/shard_map/hidden_grad/ppermute | solution.py:34
  101.7 2.7 %collective-permute-done.38.refs_3_ = bf16[4,256,256]{2,1,0:T(8,128)(2,1)S(1)} collective-permute-done((bf16[4,256,256]{2,1,0:T(8,128)(2,1)S(1)}, bf16[4,256,256]{2,1,0:T(8,128)(2,1)S(1)}, u32[]{:S(2)}, u32[]{:S(2)}) %collective-permute-start.38) | collective-permute-done | bytes 524320 | tf_op jit(solution)/shard_map/hidden_grad/ppermute | solution.py:34
  105.2 2.5 %collective-permute-start.40 = (bf16[256,256]{1,0:T(8,128)(2,1)S(1)}, bf16[256,256]{1,0:T(8,128)(2,1)S(1)}, u32[]{:S(2)}, u32[]{:S(2)}) collective-permute-start(bf16[256,256]{1,0:T(8,128)(2,1)S(1)} %get-tuple-element.122), channel_id=1, source_target_pairs={{0,4},{1,17},{2,6},{3,19},{4,0},{5,21},{6,2},{7,23},{8,12},{9,25},... | collective-permute-start | bytes 393224 | tf_op jit(solution)/shard_map/reduce_second/ppermute | solution.py:34
  115.4 3.8 %collective-permute-start.44 = (bf16[64,256]{1,0:T(8,128)(2,1)S(1)}, bf16[64,256]{1,0:T(8,128)(2,1)S(1)}, u32[]{:S(2)}, u32[]{:S(2)}) collective-permute-start(bf16[64,256]{1,0:T(8,128)(2,1)S(1)} %get-tuple-element.126), channel_id=1, source_target_pairs={{0,192},{1,65},{2,194},{3,67},{4,196},{5,69},{6,198},{7,71},{8,200... | collective-permute-start | bytes 98312 | tf_op jit(solution)/shard_map/reduce_tok/ppermute | solution.py:34
  123.6 4.8 %collective-permute-start.46 = (bf16[64,128]{1,0:T(8,128)(2,1)S(1)}, bf16[64,128]{1,0:T(8,128)(2,1)S(1)}, u32[]{:S(2)}, u32[]{:S(2)}) collective-permute-start(bf16[64,128]{1,0:T(8,128)(2,1)S(1)} %get-tuple-element.129), channel_id=1, source_target_pairs={{0,1},{1,0},{2,3},{3,2},{4,5},{5,4},{6,7},{7,6},{8,9},{9,8},{10,11... | collective-permute-start | bytes 49160 | tf_op jit(solution)/shard_map/hidden_out/ppermute | solution.py:30
  (100 shorter events, 53.8 us)
Async XLA Ops:
  0.6 16.7 %collective-permute-start = (bf16[64,256]{1,0:T(8,128)(2,1)}, bf16[64,256]{1,0:T(8,128)(2,1)S(1)}, u32[]{:S(2)}, u32[]{:S(2)}) collective-permute-start(bf16[64,256]{1,0:T(8,128)(2,1)} %bitcast.28), channel_id=1, source_target_pairs={{0,32},{1,33},{2,34},{3,35},{4,36},{5,37},{6,38},{7,39},{8,40},{9,... | collective-permute-start | bytes 98312 | tf_op jit(solution)/shard_map/gather_tok/ppermute | solution.py:30
  4.5 12.8 %collective-permute-start.1 = (bf16[64,256]{1,0:T(8,128)(2,1)}, bf16[64,256]{1,0:T(8,128)(2,1)S(1)}, u32[]{:S(2)}, u32[]{:S(2)}) collective-permute-start(bf16[64,256]{1,0:T(8,128)(2,1)} %bitcast.29), channel_id=1, source_target_pairs={{0,64},{1,65},{2,66},{3,67},{4,68},{5,69},{6,70},{7,71},{8,72},{9,... | collective-permute-start | bytes 98312 | tf_op jit(solution)/shard_map/gather_tok/ppermute | solution.py:30
  9.6 7.7 %collective-permute-start.2 = (bf16[64,256]{1,0:T(8,128)(2,1)}, bf16[64,256]{1,0:T(8,128)(2,1)S(1)}, u32[]{:S(2)}, u32[]{:S(2)}) collective-permute-start(bf16[64,256]{1,0:T(8,128)(2,1)} %bitcast.30), channel_id=1, source_target_pairs={{0,96},{1,97},{2,98},{3,99},{4,100},{5,101},{6,102},{7,103},{8,104... | collective-permute-start | bytes 98312 | tf_op jit(solution)/shard_map/gather_tok/ppermute | solution.py:30
  17.4 7.3 %collective-permute-start.3 = (bf16[4,64,256]{2,1,0:T(8,128)(2,1)S(1)}, bf16[4,64,256]{2,1,0:T(8,128)(2,1)S(1)}, u32[]{:S(2)}, u32[]{:S(2)}) collective-permute-start(bf16[4,64,256]{2,1,0:T(8,128)(2,1)S(1)} %get-tuple-element.131), channel_id=1, source_target_pairs={{0,8},{1,3},{2,10},{3,5},{4,12},{5,7},{6,14},{7,1},{8,16},{9,11},{... | collective-permute-start | bytes 393224 | tf_op jit(solution)/shard_map/gather_first/ppermute | solution.py:34
  18.8 6.4 %collective-permute-start.4 = (bf16[4,64,256]{2,1,0:T(8,128)(2,1)S(1)}, bf16[4,64,256]{2,1,0:T(8,128)(2,1)S(1)}, u32[]{:S(2)}, u32[]{:S(2)}) collective-permute-start(bf16[4,64,256]{2,1,0:T(8,128)(2,1)S(1)} %get-tuple-element.131), channel_id=1, source_target_pairs={{0,16},{1,5},{2,18},{3,7},{4,20},{5,1},{6,22},{7,3},{8,24},{9,13},... | collective-permute-start | bytes 393224 | tf_op jit(solution)/shard_map/gather_first/ppermute | solution.py:34
  21.4 6.2 %collective-permute-start.5 = (bf16[4,64,256]{2,1,0:T(8,128)(2,1)S(1)}, bf16[4,64,256]{2,1,0:T(8,128)(2,1)S(1)}, u32[]{:S(2)}, u32[]{:S(2)}) collective-permute-start(bf16[4,64,256]{2,1,0:T(8,128)(2,1)S(1)} %get-tuple-element.131), channel_id=1, source_target_pairs={{0,24},{1,7},{2,26},{3,1},{4,28},{5,3},{6,30},{7,5},{8,0},{9,15},{... | collective-permute-start | bytes 393224 | tf_op jit(solution)/shard_map/gather_first/ppermute | solution.py:34
  24.7 7.2 %collective-permute-start.12 = (bf16[501,512]{1,0:T(8,128)(2,1)S(1)}, bf16[501,512]{1,0:T(8,128)(2,1)S(1)}, u32[]{:S(2)}, u32[]{:S(2)}) collective-permute-start(bf16[501,512]{1,0:T(8,128)(2,1)S(1)} %get-tuple-element.75), channel_id=1, source_target_pairs={{0,1},{1,0},{2,3},{3,2},{4,5},{5,4},{6,7},{7,6},{8,9},{9,8},{10,11... | collective-permute-start | bytes 1539080 | tf_op jit(solution)/shard_map/stage/ppermute | solution.py:30
  25.2 7.7 %collective-permute-start.13 = (bf16[501,512]{1,0:T(8,128)(2,1)S(1)}, bf16[501,512]{1,0:T(8,128)(2,1)S(1)}, u32[]{:S(2)}, u32[]{:S(2)}) collective-permute-start(bf16[501,512]{1,0:T(8,128)(2,1)S(1)} %get-tuple-element.76), channel_id=1, source_target_pairs={{0,1},{1,0},{2,3},{3,2},{4,5},{5,4},{6,7},{7,6},{8,9},{9,8},{10,11... | collective-permute-start | bytes 1539080 | tf_op jit(solution)/shard_map/stage/ppermute | solution.py:30
  28.3 9.6 %collective-permute-start.8 = (bf16[4,4,64,256]{3,2,1,0:T(8,128)(2,1)S(1)}, bf16[4,4,64,256]{3,2,1,0:T(8,128)(2,1)S(1)}, u32[]{:S(2)}, u32[]{:S(2)}) collective-permute-start(bf16[4,4,64,256]{3,2,1,0:T(8,128)(2,1)S(1)} %pad_maximum_fusion.refs_0_), channel_id=1, source_target_pairs={{0,2},{1,9},{2,4},{3,11},{4,6},{5,13},{6,0},{7,15},{8,10},{9,17},{... | collective-permute-start | bytes 1572872 | tf_op jit(solution)/shard_map/gather_second/ppermute | solution.py:34
  29.4 15.0 %collective-permute-start.18 = (bf16[4,4,64,256]{3,2,1,0:T(8,128)(2,1)S(1)}, bf16[4,4,64,256]{3,2,1,0:T(8,128)(2,1)S(1)}, u32[]{:S(2)}, u32[]{:S(2)}) collective-permute-start(bf16[4,4,64,256]{3,2,1,0:T(8,128)(2,1)S(1)} %pad_maximum_fusion.refs_0_), channel_id=1, source_target_pairs={{0,4},{1,17},{2,6},{3,19},{4,0},{5,21},{6,2},{7,23},{8,12},{9,25},... | collective-permute-start | bytes 1572872 | tf_op jit(solution)/shard_map/gather_second/ppermute | solution.py:34
  34.4 11.2 %collective-permute-start.6 = (bf16[4,4,64,256]{3,2,1,0:T(8,128)(2,1)S(1)}, bf16[4,4,64,256]{3,2,1,0:T(8,128)(2,1)S(1)}, u32[]{:S(2)}, u32[]{:S(2)}) collective-permute-start(bf16[4,4,64,256]{3,2,1,0:T(8,128)(2,1)S(1)} %pad_maximum_fusion.refs_0_), channel_id=1, source_target_pairs={{0,6},{1,25},{2,0},{3,27},{4,2},{5,29},{6,4},{7,31},{8,14},{9,1},{... | collective-permute-start | bytes 1572872 | tf_op jit(solution)/shard_map/gather_second/ppermute | solution.py:34
  36.7 8.9 %collective-permute-start.7 = (bf16[4,4,64,256]{3,2,1,0:T(8,128)(2,1)S(1)}, bf16[4,4,64,256]{3,2,1,0:T(8,128)(2,1)S(1)}, u32[]{:S(2)}, u32[]{:S(2)}) collective-permute-start(bf16[4,4,64,256]{3,2,1,0:T(8,128)(2,1)S(1)} %pad_maximum_fusion.refs_0_), channel_id=1, source_target_pairs={{0,1},{1,0},{2,3},{3,2},{4,5},{5,4},{6,7},{7,6},{8,9},{9,8},{10,11... | collective-permute-start | bytes 1572872 | tf_op jit(solution)/shard_map/gather_cores/ppermute | solution.py:30
  37.9 7.7 %collective-permute-start.17 = (bf16[4,4,64,256]{3,2,1,0:T(8,128)(2,1)S(1)}, bf16[4,4,64,256]{3,2,1,0:T(8,128)(2,1)S(1)}, u32[]{:S(2)}, u32[]{:S(2)}) collective-permute-start(bf16[4,4,64,256]{3,2,1,0:T(8,128)(2,1)S(1)} %collective-permute-done.8.refs_1_), channel_id=1, source_target_pairs={{0,1},{1,0},{2,3},{3,2},{4,5},{5,4},{6,7},{7,6},{8,9},{9,8},{10,11... | collective-permute-start | bytes 1572872 | tf_op jit(solution)/shard_map/gather_cores/ppermute | solution.py:30
  47.9 15.4 %collective-permute-start.26 = (bf16[2,256,1024]{2,1,0:T(8,128)(2,1)S(1)}, bf16[2,256,1024]{2,1,0:T(8,128)(2,1)S(1)}, u32[]{:S(2)}, u32[]{:S(2)}) collective-permute-start(bf16[2,256,1024]{2,1,0:T(8,128)(2,1)S(1)} %student_hidden.1), channel_id=1, source_target_pairs={{0,128},{1,225},{2,130},{3,227},{4,132},{5,229},{6,134},{7,231},{8... | collective-permute-start | bytes 3145736 | tf_op jit(solution)/shard_map/student_hidden/ppermute | solution.py:41
  63.3 19.3 %collective-permute-start.34 = (bf16[2,256,1024]{2,1,0:T(8,128)(2,1)S(1)}, bf16[2,256,1024]{2,1,0:T(8,128)(2,1)S(1)}, u32[]{:S(2)}, u32[]{:S(2)}) collective-permute-start(bf16[2,256,1024]{2,1,0:T(8,128)(2,1)S(1)} %collective-permute-done.26.sent_ref), channel_id=1, source_target_pairs={{0,1},{1,0},{2,3},{3,2},{4,5},{5,4},{6,7},{7,6},{8,9},{9,8},{10,11... | collective-permute-start | bytes 3145736 | tf_op jit(solution)/shard_map/student_hidden/ppermute | solution.py:30
  63.6 15.7 %collective-permute-start.22 = (bf16[501,256]{1,0:T(8,128)(2,1)S(1)}, bf16[501,256]{1,0:T(8,128)(2,1)S(1)}, u32[]{:S(2)}, u32[]{:S(2)}) collective-permute-start(bf16[501,256]{1,0:T(8,128)(2,1)S(1)} %get-tuple-element.89), channel_id=1, source_target_pairs={{0,128},{1,129},{2,130},{3,131},{4,132},{5,133},{6,134},{7,135},{8... | collective-permute-start | bytes 769544 | tf_op jit(solution)/shard_map/exchange_scaled/ppermute | solution.py:30
  72.6 6.4 %collective-permute-start.30 = (f32[8,256]{1,0:T(8,128)S(1)}, f32[8,256]{1,0:T(8,128)S(1)}, u32[]{:S(2)}, u32[]{:S(2)}) collective-permute-start(f32[8,256]{1,0:T(8,128)S(1)} %stats.6.refs_0_), channel_id=1, source_target_pairs={{0,64},{1,65},{2,66},{3,67},{4,68},{5,69},{6,70},{7,71},{8,72},{9,... | collective-permute-start | bytes 24584 | tf_op jit(solution)/shard_map/stats/ppermute | solution.py:30
  85.8 10.9 %collective-permute-start.37 = (bf16[4,256,256]{2,1,0:T(8,128)(2,1)S(1)}, bf16[4,256,256]{2,1,0:T(8,128)(2,1)S(1)}, u32[]{:S(2)}, u32[]{:S(2)}) collective-permute-start(bf16[4,256,256]{2,1,0:T(8,128)(2,1)S(1)} %hidden_grad.6), channel_id=1, source_target_pairs={{0,8},{1,3},{2,10},{3,5},{4,12},{5,7},{6,14},{7,1},{8,16},{9,11},{... | collective-permute-start | bytes 1572872 | tf_op jit(solution)/shard_map/hidden_grad/ppermute | solution.py:34
  88.9 12.8 %collective-permute-start.36 = (bf16[4,256,256]{2,1,0:T(8,128)(2,1)S(1)}, bf16[4,256,256]{2,1,0:T(8,128)(2,1)S(1)}, u32[]{:S(2)}, u32[]{:S(2)}) collective-permute-start(bf16[4,256,256]{2,1,0:T(8,128)(2,1)S(1)} %hidden_grad.7), channel_id=1, source_target_pairs={{0,16},{1,5},{2,18},{3,7},{4,20},{5,1},{6,22},{7,3},{8,24},{9,13},... | collective-permute-start | bytes 1572872 | tf_op jit(solution)/shard_map/hidden_grad/ppermute | solution.py:34
  91.8 12.5 %collective-permute-start.38 = (bf16[4,256,256]{2,1,0:T(8,128)(2,1)S(1)}, bf16[4,256,256]{2,1,0:T(8,128)(2,1)S(1)}, u32[]{:S(2)}, u32[]{:S(2)}) collective-permute-start(bf16[4,256,256]{2,1,0:T(8,128)(2,1)S(1)} %hidden_grad.8), channel_id=1, source_target_pairs={{0,24},{1,7},{2,26},{3,1},{4,28},{5,3},{6,30},{7,5},{8,0},{9,15},{... | collective-permute-start | bytes 1572872 | tf_op jit(solution)/shard_map/hidden_grad/ppermute | solution.py:34
  105.2 6.3 %collective-permute-start.40 = (bf16[256,256]{1,0:T(8,128)(2,1)S(1)}, bf16[256,256]{1,0:T(8,128)(2,1)S(1)}, u32[]{:S(2)}, u32[]{:S(2)}) collective-permute-start(bf16[256,256]{1,0:T(8,128)(2,1)S(1)} %get-tuple-element.122), channel_id=1, source_target_pairs={{0,4},{1,17},{2,6},{3,19},{4,0},{5,21},{6,2},{7,23},{8,12},{9,25},... | collective-permute-start | bytes 393224 | tf_op jit(solution)/shard_map/reduce_second/ppermute | solution.py:34
  112.6 7.8 %collective-permute-start.42 = (bf16[64,256]{1,0:T(8,128)(2,1)S(1)}, bf16[64,256]{1,0:T(8,128)(2,1)S(1)}, u32[]{:S(2)}, u32[]{:S(2)}) collective-permute-start(bf16[64,256]{1,0:T(8,128)(2,1)S(1)} %get-tuple-element.124.own_ref), channel_id=1, source_target_pairs={{0,128},{1,129},{2,130},{3,131},{4,132},{5,133},{6,134},{7,135},{8... | collective-permute-start | bytes 98312 | tf_op jit(solution)/shard_map/reduce_tok/ppermute | solution.py:30
  114.2 6.2 %collective-permute-start.43 = (bf16[64,256]{1,0:T(8,128)(2,1)S(1)}, bf16[64,256]{1,0:T(8,128)(2,1)S(1)}, u32[]{:S(2)}, u32[]{:S(2)}) collective-permute-start(bf16[64,256]{1,0:T(8,128)(2,1)S(1)} %get-tuple-element.125), channel_id=1, source_target_pairs={{0,160},{1,33},{2,162},{3,35},{4,164},{5,37},{6,166},{7,39},{8,168... | collective-permute-start | bytes 98312 | tf_op jit(solution)/shard_map/reduce_tok/ppermute | solution.py:34
  115.4 6.9 %collective-permute-start.44 = (bf16[64,256]{1,0:T(8,128)(2,1)S(1)}, bf16[64,256]{1,0:T(8,128)(2,1)S(1)}, u32[]{:S(2)}, u32[]{:S(2)}) collective-permute-start(bf16[64,256]{1,0:T(8,128)(2,1)S(1)} %get-tuple-element.126), channel_id=1, source_target_pairs={{0,192},{1,65},{2,194},{3,67},{4,196},{5,69},{6,198},{7,71},{8,200... | collective-permute-start | bytes 98312 | tf_op jit(solution)/shard_map/reduce_tok/ppermute | solution.py:34
  (27 other events, 152.2 us)
where the time goes:
time: 131 us; the launch traced here: 130 us
  starting transfers between devices  72.2 us (55%)
  waiting for transfers between devices  31.5 us (24%)
  Pallas kernels  22.3 us (17%)
  local copies, waits for them, and re-layouts  3.44 us (3%)
    ppermute x28, starting transfers between devices, send(): return lax.ppermute(block, AXES, route(lambda place: shift))  40.8 us
    ppermute x18, starting transfers between devices, send_by_core(): lax.ppermute(block, AXES, route(lambda place: odd if place['c'] else even))  31.1 us
    ppermute x18, waiting for transfers between devices, send_by_core(): lax.ppermute(block, AXES, route(lambda place: odd if place['c'] else even))  19.9 us
    ppermute x28, waiting for transfers between devices, send(): return lax.ppermute(block, AXES, route(lambda place: shift))  11.6 us
    pallas_call x4, Pallas kernels, products(): pl.pallas_call(functools.partial(products_kernel, d), out_shape=jax.Shape...  4.8 us
    pallas_call x1, Pallas kernels, head_grad_half(): pl.pallas_call(head_grad_kernel, grid_spec=pltpu.PrefetchScalarGridSpec(n...  4.36 us
    unnamed x8, local copies, waits for them, and re-layouts  3.36 us
    pallas_call x1, Pallas kernels, logits_parts(): pl.pallas_call(logits_kernel, out_shape=[jax.ShapeDtypeStruct((4, toks, 4...  3.16 us
  transfers between devices with their start and end apart: 47, of which 21 were waited for; matrix products, arithmetic and copies ran while one was open for 0% of the time, Pallas kernels for 14%

commit v1 on v0

--- a/solution.py
+++ b/solution.py
@@ -543,14 +543,13 @@
         for d in (1, 2, 3, 0):
             parts = (part,) if d == 1 else ()
             if d == 0:
-                turned, firsts[0] = lax.optimization_barrier((turned, firsts[0]))
+                grad, firsts[0] = lax.optimization_barrier((grad, firsts[0]))
+                head_out = head_grad_half(place, grad, hidden_own, hidden_other, sent, twin)
+                turned, firsts[1], head_out = lax.optimization_barrier((turned, firsts[1], head_out))
             sums.append(products(place, turned, head_t, turned_twin, halves[2 * d : 2 * d + 2], d, *parts))
             turned, sums[-1] = lax.optimization_barrier((turned, sums[-1]))
             if d > 0:
                 firsts.append(send_by_core(sums[-1], {"x": d}, {"y": d}))
-    with jax.named_scope("head_grad"):
-        head_out = head_grad_half(place, grad, hidden_own, hidden_other, sent, twin)
-        firsts[1], head_out = lax.optimization_barrier((firsts[1], head_out))
     with jax.named_scope("reduce_second"):
         parts = add_split(sums[3], *firsts)
         seconds = [send_by_core(parts[d], {"y": d}, {"x": d}) for d in (1, 2, 3)]

time: 131 us -> 131 us (level)
  transfers between devices with their start and end apart: 47 -> 47, of which waited for: 21 -> 24; matrix products, arithmetic and copies ran while one was open for 0% -> 0% of each run, Pallas kernels for 14% -> 14%
where the time goes in v1:
time: 131 us; the launch traced here: 129 us
  starting transfers between devices  72.1 us (55%)
  waiting for transfers between devices  30.5 us (23%)
  Pallas kernels  22.4 us (17%)
  local copies, waits for them, and re-layouts  3.44 us (3%)
    ppermute x28, starting transfers between devices, send(): return lax.ppermute(block, AXES, route(lambda place: shift))  39.7 us
    ppermute x18, starting transfers between devices, send_by_core(): lax.ppermute(block, AXES, route(lambda place: odd if place['c'] else even))  31.3 us
    ppermute x18, waiting for transfers between devices, send_by_core(): lax.ppermute(block, AXES, route(lambda place: odd if place['c'] else even))  18.7 us
    ppermute x28, waiting for transfers between devices, send(): return lax.ppermute(block, AXES, route(lambda place: shift))  11.8 us
    pallas_call x4, Pallas kernels, products(): pl.pallas_call(functools.partial(products_kernel, d), out_shape=jax.Shape...  4.79 us
    pallas_call x1, Pallas kernels, head_grad_half(): pl.pallas_call(head_grad_kernel, grid_spec=pltpu.PrefetchScalarGridSpec(n...  4.37 us
    unnamed x8, local copies, waits for them, and re-layouts  3.36 us
    pallas_call x1, Pallas kernels, logits_parts(): pl.pallas_call(logits_kernel, out_shape=[jax.ShapeDtypeStruct((4, toks, 4...  3.16 us
  transfers between devices with their start and end apart: 47, of which 24 were waited for; matrix products, arithmetic and copies ran while one was open for 0% of the time, Pallas kernels for 14%

profile of v1, /device:TPU:1, one launch (start us, length us, event | category | flops | bytes accessed | tf_op | source)
XLA Modules:
  0.0 129.3 jit_solution(14953447500263667576)
XLA Ops:
  0.6 6.9 %collective-permute-start.2 = (bf16[64,256]{1,0:T(8,128)(2,1)}, bf16[64,256]{1,0:T(8,128)(2,1)S(1)}, u32[]{:S(2)}, u32[]{:S(2)}) collective-permute-start(bf16[64,256]{1,0:T(8,128)(2,1)} %bitcast.28), channel_id=1, source_target_pairs={{0,96},{1,97},{2,98},{3,99},{4,100},{5,101},{6,102},{7,103},{8,104... | collective-permute-start | bytes 98312 | tf_op jit(solution)/shard_map/gather_tok/ppermute | solution.py:30
  8.5 2.3 %collective-permute-start = (bf16[64,256]{1,0:T(8,128)(2,1)}, bf16[64,256]{1,0:T(8,128)(2,1)S(1)}, u32[]{:S(2)}, u32[]{:S(2)}) collective-permute-start(bf16[64,256]{1,0:T(8,128)(2,1)} %bitcast.30), channel_id=1, source_target_pairs={{0,32},{1,33},{2,34},{3,35},{4,36},{5,37},{6,38},{7,39},{8,40},{9,... | collective-permute-start | bytes 98312 | tf_op jit(solution)/shard_map/gather_tok/ppermute | solution.py:30
  10.9 3.3 %copy-done = bf16[1,8192,501]{1,2,0:T(8,128)(2,1)S(1)} copy-done((bf16[1,8192,501]{1,2,0:T(8,128)(2,1)S(1)}, bf16[1,8192,501]{1,2,0:T(8,128)(2,1)}, u32[]{:S(2)}) %copy-start) | copy-done | bytes 8208408
  14.2 1.9 %stage.1 = (bf16[501,8192]{1,0:T(8,128)(2,1)S(1)}, bf16[501,512]{1,0:T(8,128)(2,1)S(1)}, bf16[501,512]{1,0:T(8,128)(2,1)S(1)}, bf16[501,512]{1,0:T(8,128)(2,1)S(...) custom-call(s32[5]{0:T(128)S(1)} %stack.53.place_ref, ...), custom_call_target="tpu_custom_call" | custom-call | tf_op jit(solution)/shard_map/stage/pallas_call | solution.py:72
  16.2 3.0 %collective-permute-start.4 = (bf16[4,64,256]{2,1,0:T(8,128)(2,1)S(1)}, bf16[4,64,256]{2,1,0:T(8,128)(2,1)S(1)}, u32[]{:S(2)}, u32[]{:S(2)}) collective-permute-start(bf16[4,64,256]{2,1,0:T(8,128)(2,1)S(1)} %get-tuple-element.133), channel_id=1, source_target_pairs={{0,16},{1,5},{2,18},{3,7},{4,20},{5,1},{6,22},{7,3},{8,24},{9,13},... | collective-permute-start | bytes 393224 | tf_op jit(solution)/shard_map/gather_first/ppermute | solution.py:34
  19.6 2.3 %collective-permute-start.5 = (bf16[4,64,256]{2,1,0:T(8,128)(2,1)S(1)}, bf16[4,64,256]{2,1,0:T(8,128)(2,1)S(1)}, u32[]{:S(2)}, u32[]{:S(2)}) collective-permute-start(bf16[4,64,256]{2,1,0:T(8,128)(2,1)S(1)} %get-tuple-element.133), channel_id=1, source_target_pairs={{0,24},{1,7},{2,26},{3,1},{4,28},{5,3},{6,30},{7,5},{8,0},{9,15},{... | collective-permute-start | bytes 393224 | tf_op jit(solution)/shard_map/gather_first/ppermute | solution.py:34
  21.9 2.2 %collective-permute-start.9 = (bf16[501,512]{1,0:T(8,128)(2,1)S(1)}, bf16[501,512]{1,0:T(8,128)(2,1)S(1)}, u32[]{:S(2)}, u32[]{:S(2)}) collective-permute-start(bf16[501,512]{1,0:T(8,128)(2,1)S(1)} %get-tuple-element.73), channel_id=1, source_target_pairs={{0,1},{1,0},{2,3},{3,2},{4,5},{5,4},{6,7},{7,6},{8,9},{9,8},{10,11... | collective-permute-start | bytes 1539080 | tf_op jit(solution)/shard_map/stage/ppermute | solution.py:30
  24.6 2.4 %collective-permute-start.12 = (bf16[501,512]{1,0:T(8,128)(2,1)S(1)}, bf16[501,512]{1,0:T(8,128)(2,1)S(1)}, u32[]{:S(2)}, u32[]{:S(2)}) collective-permute-start(bf16[501,512]{1,0:T(8,128)(2,1)S(1)} %get-tuple-element.76), channel_id=1, source_target_pairs={{0,1},{1,0},{2,3},{3,2},{4,5},{5,4},{6,7},{7,6},{8,9},{9,8},{10,11... | collective-permute-start | bytes 1539080 | tf_op jit(solution)/shard_map/stage/ppermute | solution.py:30
  27.2 4.1 %collective-permute-start.18 = (bf16[4,4,64,256]{3,2,1,0:T(8,128)(2,1)S(1)}, bf16[4,4,64,256]{3,2,1,0:T(8,128)(2,1)S(1)}, u32[]{:S(2)}, u32[]{:S(2)}) collective-permute-start(bf16[4,4,64,256]{3,2,1,0:T(8,128)(2,1)S(1)} %pad_maximum_fusion.refs_0_), channel_id=1, source_target_pairs={{0,4},{1,17},{2,6},{3,19},{4,0},{5,21},{6,2},{7,23},{8,12},{9,25},... | collective-permute-start | bytes 1572872 | tf_op jit(solution)/shard_map/gather_second/ppermute | solution.py:34
  34.4 2.4 %collective-permute-start.6 = (bf16[4,4,64,256]{3,2,1,0:T(8,128)(2,1)S(1)}, bf16[4,4,64,256]{3,2,1,0:T(8,128)(2,1)S(1)}, u32[]{:S(2)}, u32[]{:S(2)}) collective-permute-start(bf16[4,4,64,256]{3,2,1,0:T(8,128)(2,1)S(1)} %pad_maximum_fusion.refs_0_), channel_id=1, source_target_pairs={{0,6},{1,25},{2,0},{3,27},{4,2},{5,29},{6,4},{7,31},{8,14},{9,1},{... | collective-permute-start | bytes 1572872 | tf_op jit(solution)/shard_map/gather_second/ppermute | solution.py:34
  37.0 6.8 %collective-permute-done.18.refs_2_ = bf16[4,4,64,256]{3,2,1,0:T(8,128)(2,1)S(1)} collective-permute-done((bf16[4,4,64,256]{3,2,1,0:T(8,128)(2,1)S(1)}, bf16[4,4,64,256]{3,2,1,0:T(8,128)(2,1)S(1)}, u32[]{:S(2)}, u32[]{:S(2)}) %collective-permute-start.18) | collective-permute-done | bytes 524320 | tf_op jit(solution)/shard_map/gather_second/ppermute | solution.py:34
  49.5 2.9 %own_logits.1 = (bf16[4,256,1024]{2,1,0:T(8,128)(2,1)S(1)}, f32[501,256]{1,0:T(8,128)S(1)}) custom-call(s32[5]{0:T(128)S(1)} %stack.53.place_ref, bf16[501,8192]{1,0:T(8,128)(2,1)S(1)} %get-tuple-element.68.head_ref, bf16[4,4,64,256]{3,2,1,0:T(8,128)(2,1)S(1)} %pad_maximum_fusion.refs_0_, bf16[4,4,64,256]{3,2,1,0:T(8,128)(2,1)S(1)} %collective-permute-done.8.refs_1_, ...), custom_call_target="tpu_custom_call" | custom-call | tf_op jit(solution)/shard_map/own_logits/pallas_call | solution.py:162
  52.4 3.2 %logits.1 = (bf16[4,256,1024]{2,1,0:T(8,128)(2,1)S(1)}, f32[501,256]{1,0:T(8,128)S(1)}, bf16[501,256]{1,0:T(8,128)(2,1)S(1)}, f32[8,256]{1,0:T(8,128)S(1)}) custom-call(s32[5]{0:T(128)S(1)} %stack.53.place_ref, bf16[501,8192]{1,0:T(8,128)(2,1)S(1)} %get-tuple-element.68.head_ref, bf16[4,4,64,256]{3,2,1,0:T(8,128)(2,1)S(1)} %collective-permute-done.7.refs_0_, ...), custom_call_target="tpu_custom_call" | custom-call | tf_op jit(solution)/shard_map/logits/pallas_call | solution.py:195
  56.9 2.5 %collective-permute-start.24 = (f32[8,256]{1,0:T(8,128)S(1)}, f32[8,256]{1,0:T(8,128)S(1)}, u32[]{:S(2)}, u32[]{:S(2)}) collective-permute-start(f32[8,256]{1,0:T(8,128)S(1)} %stats.4.refs_0_), channel_id=1, source_target_pairs={{0,8},{1,25},{2,10},{3,27},{4,12},{5,29},{6,14},{7,31},{8,16},{9,1... | collective-permute-start | bytes 24584 | tf_op jit(solution)/shard_map/stats/ppermute | solution.py:34
  67.8 2.8 %collective-permute-start.29 = (f32[8,256]{1,0:T(8,128)S(1)}, f32[8,256]{1,0:T(8,128)S(1)}, u32[]{:S(2)}, u32[]{:S(2)}) collective-permute-start(f32[8,256]{1,0:T(8,128)S(1)} %collective-permute-done.28.refs_2_), channel_id=1, source_target_pairs={{0,1},{1,0},{2,3},{3,2},{4,5},{5,4},{6,7},{7,6},{8,9},{9,8},{10,11... | collective-permute-start | bytes 24584 | tf_op jit(solution)/shard_map/stats/ppermute | solution.py:30
  72.7 3.8 %collective-permute-start.30 = (f32[8,256]{1,0:T(8,128)S(1)}, f32[8,256]{1,0:T(8,128)S(1)}, u32[]{:S(2)}, u32[]{:S(2)}) collective-permute-start(f32[8,256]{1,0:T(8,128)S(1)} %stats.6.refs_0_), channel_id=1, source_target_pairs={{0,64},{1,65},{2,66},{3,67},{4,68},{5,69},{6,70},{7,71},{8,72},{9,... | collective-permute-start | bytes 24584 | tf_op jit(solution)/shard_map/stats/ppermute | solution.py:30
  79.8 2.1 %collective-permute-done.33.other_stats = f32[8,256]{1,0:T(8,128)S(1)} collective-permute-done((f32[8,256]{1,0:T(8,128)S(1)}, f32[8,256]{1,0:T(8,128)S(1)}, u32[]{:S(2)}, u32[]{:S(2)}) %collective-permute-start.33) | collective-permute-done | bytes 8224 | tf_op jit(solution)/shard_map/stats/ppermute | solution.py:30
  82.7 3.6 %collective-permute-start.35 = (bf16[256,501]{1,0:T(8,128)(2,1)S(1)}, bf16[256,501]{1,0:T(8,128)(2,1)S(1)}, u32[]{:S(2)}, u32[]{:S(2)}) collective-permute-start(bf16[256,501]{1,0:T(8,128)(2,1)S(1)} %get-tuple-element.115.turned_ref), channel_id=1, source_target_pairs={{0,1},{1,0},{2,3},{3,2},{4,5},{5,4},{6,7},{7,6},{8,9},{9,8},{10,11... | collective-permute-start | bytes 769544 | tf_op jit(solution)/shard_map/hidden_grad/ppermute | solution.py:30
  90.1 3.0 %collective-permute-start.36 = (bf16[4,256,256]{2,1,0:T(8,128)(2,1)S(1)}, bf16[4,256,256]{2,1,0:T(8,128)(2,1)S(1)}, u32[]{:S(2)}, u32[]{:S(2)}) collective-permute-start(bf16[4,256,256]{2,1,0:T(8,128)(2,1)S(1)} %hidden_grad.8), channel_id=1, source_target_pairs={{0,16},{1,5},{2,18},{3,7},{4,20},{5,1},{6,22},{7,3},{8,24},{9,13},... | collective-permute-start | bytes 1572872 | tf_op jit(solution)/shard_map/hidden_grad/ppermute | solution.py:34
  95.0 3.1 %collective-permute-done.37.refs_1_ = bf16[4,256,256]{2,1,0:T(8,128)(2,1)S(1)} collective-permute-done((bf16[4,256,256]{2,1,0:T(8,128)(2,1)S(1)}, bf16[4,256,256]{2,1,0:T(8,128)(2,1)S(1)}, u32[]{:S(2)}, u32[]{:S(2)}) %collective-permute-start.37) | collective-permute-done | bytes 524320 | tf_op jit(solution)/shard_map/hidden_grad/ppermute | solution.py:34
  98.0 4.4 %hidden_grad.10 = bf16[501,4096]{1,0:T(8,128)(2,1)} custom-call(s32[5]{0:T(128)S(1)} %stack.53.place_ref, bf16[501,256]{1,0:T(8,128)(2,1)S(1)} %get-tuple-element.110.grad_ref, bf16[4,256,1024]{2,1,0:T(8,128)(2,1)S(1)} %get-tuple-element.111.own_ref, bf16[4,256,1024]{2,1,0:T(8,128)(2,1)S(1)} %get-tuple-element.112.other_ref, ...), custom_call_target="tpu_custom_call" | custom-call | tf_op jit(solution)/shard_map/hidden_grad/pallas_call | solution.py:461
  106.0 3.0 %collective-permute-start.40 = (bf16[256,256]{1,0:T(8,128)(2,1)S(1)}, bf16[256,256]{1,0:T(8,128)(2,1)S(1)}, u32[]{:S(2)}, u32[]{:S(2)}) collective-permute-start(bf16[256,256]{1,0:T(8,128)(2,1)S(1)} %get-tuple-element.124), channel_id=1, source_target_pairs={{0,4},{1,17},{2,6},{3,19},{4,0},{5,21},{6,2},{7,23},{8,12},{9,25},... | collective-permute-start | bytes 393224 | tf_op jit(solution)/shard_map/reduce_second/ppermute | solution.py:34
  114.9 3.1 %collective-permute-start.44 = (bf16[64,256]{1,0:T(8,128)(2,1)S(1)}, bf16[64,256]{1,0:T(8,128)(2,1)S(1)}, u32[]{:S(2)}, u32[]{:S(2)}) collective-permute-start(bf16[64,256]{1,0:T(8,128)(2,1)S(1)} %get-tuple-element.128), channel_id=1, source_target_pairs={{0,192},{1,65},{2,194},{3,67},{4,196},{5,69},{6,198},{7,71},{8,200... | collective-permute-start | bytes 98312 | tf_op jit(solution)/shard_map/reduce_tok/ppermute | solution.py:34
  122.9 4.4 %collective-permute-start.46 = (bf16[64,128]{1,0:T(8,128)(2,1)S(1)}, bf16[64,128]{1,0:T(8,128)(2,1)S(1)}, u32[]{:S(2)}, u32[]{:S(2)}) collective-permute-start(bf16[64,128]{1,0:T(8,128)(2,1)S(1)} %get-tuple-element.131), channel_id=1, source_target_pairs={{0,1},{1,0},{2,3},{3,2},{4,5},{5,4},{6,7},{7,6},{8,9},{9,8},{10,11... | collective-permute-start | bytes 49160 | tf_op jit(solution)/shard_map/hidden_out/ppermute | solution.py:30
  (100 shorter events, 48.9 us)
Async XLA Ops:
  0.6 15.5 %collective-permute-start.2 = (bf16[64,256]{1,0:T(8,128)(2,1)}, bf16[64,256]{1,0:T(8,128)(2,1)S(1)}, u32[]{:S(2)}, u32[]{:S(2)}) collective-permute-start(bf16[64,256]{1,0:T(8,128)(2,1)} %bitcast.28), channel_id=1, source_target_pairs={{0,96},{1,97},{2,98},{3,99},{4,100},{5,101},{6,102},{7,103},{8,104... | collective-permute-start | bytes 98312 | tf_op jit(solution)/shard_map/gather_tok/ppermute | solution.py:30
  7.6 8.6 %collective-permute-start.1 = (bf16[64,256]{1,0:T(8,128)(2,1)}, bf16[64,256]{1,0:T(8,128)(2,1)S(1)}, u32[]{:S(2)}, u32[]{:S(2)}) collective-permute-start(bf16[64,256]{1,0:T(8,128)(2,1)} %bitcast.29), channel_id=1, source_target_pairs={{0,64},{1,65},{2,66},{3,67},{4,68},{5,69},{6,70},{7,71},{8,72},{9,... | collective-permute-start | bytes 98312 | tf_op jit(solution)/shard_map/gather_tok/ppermute | solution.py:30
  8.5 7.6 %collective-permute-start = (bf16[64,256]{1,0:T(8,128)(2,1)}, bf16[64,256]{1,0:T(8,128)(2,1)S(1)}, u32[]{:S(2)}, u32[]{:S(2)}) collective-permute-start(bf16[64,256]{1,0:T(8,128)(2,1)} %bitcast.30), channel_id=1, source_target_pairs={{0,32},{1,33},{2,34},{3,35},{4,36},{5,37},{6,38},{7,39},{8,40},{9,... | collective-permute-start | bytes 98312 | tf_op jit(solution)/shard_map/gather_tok/ppermute | solution.py:30
  16.2 7.8 %collective-permute-start.4 = (bf16[4,64,256]{2,1,0:T(8,128)(2,1)S(1)}, bf16[4,64,256]{2,1,0:T(8,128)(2,1)S(1)}, u32[]{:S(2)}, u32[]{:S(2)}) collective-permute-start(bf16[4,64,256]{2,1,0:T(8,128)(2,1)S(1)} %get-tuple-element.133), channel_id=1, source_target_pairs={{0,16},{1,5},{2,18},{3,7},{4,20},{5,1},{6,22},{7,3},{8,24},{9,13},... | collective-permute-start | bytes 393224 | tf_op jit(solution)/shard_map/gather_first/ppermute | solution.py:34
  19.2 5.4 %collective-permute-start.3 = (bf16[4,64,256]{2,1,0:T(8,128)(2,1)S(1)}, bf16[4,64,256]{2,1,0:T(8,128)(2,1)S(1)}, u32[]{:S(2)}, u32[]{:S(2)}) collective-permute-start(bf16[4,64,256]{2,1,0:T(8,128)(2,1)S(1)} %get-tuple-element.133), channel_id=1, source_target_pairs={{0,8},{1,3},{2,10},{3,5},{4,12},{5,7},{6,14},{7,1},{8,16},{9,11},{... | collective-permute-start | bytes 393224 | tf_op jit(solution)/shard_map/gather_first/ppermute | solution.py:34
  19.6 7.5 %collective-permute-start.5 = (bf16[4,64,256]{2,1,0:T(8,128)(2,1)S(1)}, bf16[4,64,256]{2,1,0:T(8,128)(2,1)S(1)}, u32[]{:S(2)}, u32[]{:S(2)}) collective-permute-start(bf16[4,64,256]{2,1,0:T(8,128)(2,1)S(1)} %get-tuple-element.133), channel_id=1, source_target_pairs={{0,24},{1,7},{2,26},{3,1},{4,28},{5,3},{6,30},{7,5},{8,0},{9,15},{... | collective-permute-start | bytes 393224 | tf_op jit(solution)/shard_map/gather_first/ppermute | solution.py:34
  24.1 7.2 %collective-permute-start.11 = (bf16[501,512]{1,0:T(8,128)(2,1)S(1)}, bf16[501,512]{1,0:T(8,128)(2,1)S(1)}, u32[]{:S(2)}, u32[]{:S(2)}) collective-permute-start(bf16[501,512]{1,0:T(8,128)(2,1)S(1)} %get-tuple-element.75), channel_id=1, source_target_pairs={{0,1},{1,0},{2,3},{3,2},{4,5},{5,4},{6,7},{7,6},{8,9},{9,8},{10,11... | collective-permute-start | bytes 1539080 | tf_op jit(solution)/shard_map/stage/ppermute | solution.py:30
  24.6 7.6 %collective-permute-start.12 = (bf16[501,512]{1,0:T(8,128)(2,1)S(1)}, bf16[501,512]{1,0:T(8,128)(2,1)S(1)}, u32[]{:S(2)}, u32[]{:S(2)}) collective-permute-start(bf16[501,512]{1,0:T(8,128)(2,1)S(1)} %get-tuple-element.76), channel_id=1, source_target_pairs={{0,1},{1,0},{2,3},{3,2},{4,5},{5,4},{6,7},{7,6},{8,9},{9,8},{10,11... | collective-permute-start | bytes 1539080 | tf_op jit(solution)/shard_map/stage/ppermute | solution.py:30
  27.0 5.3 %collective-permute-start.13 = (bf16[501,512]{1,0:T(8,128)(2,1)S(1)}, bf16[501,512]{1,0:T(8,128)(2,1)S(1)}, u32[]{:S(2)}, u32[]{:S(2)}) collective-permute-start(bf16[501,512]{1,0:T(8,128)(2,1)S(1)} %get-tuple-element.77), channel_id=1, source_target_pairs={{0,1},{1,0},{2,3},{3,2},{4,5},{5,4},{6,7},{7,6},{8,9},{9,8},{10,11... | collective-permute-start | bytes 1539080 | tf_op jit(solution)/shard_map/stage/ppermute | solution.py:30
  27.1 9.9 %collective-permute-start.8 = (bf16[4,4,64,256]{3,2,1,0:T(8,128)(2,1)S(1)}, bf16[4,4,64,256]{3,2,1,0:T(8,128)(2,1)S(1)}, u32[]{:S(2)}, u32[]{:S(2)}) collective-permute-start(bf16[4,4,64,256]{3,2,1,0:T(8,128)(2,1)S(1)} %pad_maximum_fusion.refs_0_), channel_id=1, source_target_pairs={{0,2},{1,9},{2,4},{3,11},{4,6},{5,13},{6,0},{7,15},{8,10},{9,17},{... | collective-permute-start | bytes 1572872 | tf_op jit(solution)/shard_map/gather_second/ppermute | solution.py:34
  27.2 16.6 %collective-permute-start.18 = (bf16[4,4,64,256]{3,2,1,0:T(8,128)(2,1)S(1)}, bf16[4,4,64,256]{3,2,1,0:T(8,128)(2,1)S(1)}, u32[]{:S(2)}, u32[]{:S(2)}) collective-permute-start(bf16[4,4,64,256]{3,2,1,0:T(8,128)(2,1)S(1)} %pad_maximum_fusion.refs_0_), channel_id=1, source_target_pairs={{0,4},{1,17},{2,6},{3,19},{4,0},{5,21},{6,2},{7,23},{8,12},{9,25},... | collective-permute-start | bytes 1572872 | tf_op jit(solution)/shard_map/gather_second/ppermute | solution.py:34
  33.7 11.2 %collective-permute-start.7 = (bf16[4,4,64,256]{3,2,1,0:T(8,128)(2,1)S(1)}, bf16[4,4,64,256]{3,2,1,0:T(8,128)(2,1)S(1)}, u32[]{:S(2)}, u32[]{:S(2)}) collective-permute-start(bf16[4,4,64,256]{3,2,1,0:T(8,128)(2,1)S(1)} %pad_maximum_fusion.refs_0_), channel_id=1, source_target_pairs={{0,1},{1,0},{2,3},{3,2},{4,5},{5,4},{6,7},{7,6},{8,9},{9,8},{10,11... | collective-permute-start | bytes 1572872 | tf_op jit(solution)/shard_map/gather_cores/ppermute | solution.py:30
  34.4 10.5 %collective-permute-start.6 = (bf16[4,4,64,256]{3,2,1,0:T(8,128)(2,1)S(1)}, bf16[4,4,64,256]{3,2,1,0:T(8,128)(2,1)S(1)}, u32[]{:S(2)}, u32[]{:S(2)}) collective-permute-start(bf16[4,4,64,256]{3,2,1,0:T(8,128)(2,1)S(1)} %pad_maximum_fusion.refs_0_), channel_id=1, source_target_pairs={{0,6},{1,25},{2,0},{3,27},{4,2},{5,29},{6,4},{7,31},{8,14},{9,1},{... | collective-permute-start | bytes 1572872 | tf_op jit(solution)/shard_map/gather_second/ppermute | solution.py:34
  48.0 15.4 %collective-permute-start.26 = (bf16[2,256,1024]{2,1,0:T(8,128)(2,1)S(1)}, bf16[2,256,1024]{2,1,0:T(8,128)(2,1)S(1)}, u32[]{:S(2)}, u32[]{:S(2)}) collective-permute-start(bf16[2,256,1024]{2,1,0:T(8,128)(2,1)S(1)} %student_hidden.1), channel_id=1, source_target_pairs={{0,128},{1,225},{2,130},{3,227},{4,132},{5,229},{6,134},{7,231},{8... | collective-permute-start | bytes 3145736 | tf_op jit(solution)/shard_map/student_hidden/ppermute | solution.py:41
  63.4 19.3 %collective-permute-start.34 = (bf16[2,256,1024]{2,1,0:T(8,128)(2,1)S(1)}, bf16[2,256,1024]{2,1,0:T(8,128)(2,1)S(1)}, u32[]{:S(2)}, u32[]{:S(2)}) collective-permute-start(bf16[2,256,1024]{2,1,0:T(8,128)(2,1)S(1)} %collective-permute-done.26.sent_ref), channel_id=1, source_target_pairs={{0,1},{1,0},{2,3},{3,2},{4,5},{5,4},{6,7},{7,6},{8,9},{9,8},{10,11... | collective-permute-start | bytes 3145736 | tf_op jit(solution)/shard_map/student_hidden/ppermute | solution.py:30
  63.5 16.3 %collective-permute-start.22 = (bf16[501,256]{1,0:T(8,128)(2,1)S(1)}, bf16[501,256]{1,0:T(8,128)(2,1)S(1)}, u32[]{:S(2)}, u32[]{:S(2)}) collective-permute-start(bf16[501,256]{1,0:T(8,128)(2,1)S(1)} %get-tuple-element.90), channel_id=1, source_target_pairs={{0,128},{1,129},{2,130},{3,131},{4,132},{5,133},{6,134},{7,135},{8... | collective-permute-start | bytes 769544 | tf_op jit(solution)/shard_map/exchange_scaled/ppermute | solution.py:30
  72.7 6.4 %collective-permute-start.30 = (f32[8,256]{1,0:T(8,128)S(1)}, f32[8,256]{1,0:T(8,128)S(1)}, u32[]{:S(2)}, u32[]{:S(2)}) collective-permute-start(f32[8,256]{1,0:T(8,128)S(1)} %stats.6.refs_0_), channel_id=1, source_target_pairs={{0,64},{1,65},{2,66},{3,67},{4,68},{5,69},{6,70},{7,71},{8,72},{9,... | collective-permute-start | bytes 24584 | tf_op jit(solution)/shard_map/stats/ppermute | solution.py:30
  88.4 9.6 %collective-permute-start.37 = (bf16[4,256,256]{2,1,0:T(8,128)(2,1)S(1)}, bf16[4,256,256]{2,1,0:T(8,128)(2,1)S(1)}, u32[]{:S(2)}, u32[]{:S(2)}) collective-permute-start(bf16[4,256,256]{2,1,0:T(8,128)(2,1)S(1)} %hidden_grad.7), channel_id=1, source_target_pairs={{0,8},{1,3},{2,10},{3,5},{4,12},{5,7},{6,14},{7,1},{8,16},{9,11},{... | collective-permute-start | bytes 1572872 | tf_op jit(solution)/shard_map/hidden_grad/ppermute | solution.py:34
  90.1 14.1 %collective-permute-start.36 = (bf16[4,256,256]{2,1,0:T(8,128)(2,1)S(1)}, bf16[4,256,256]{2,1,0:T(8,128)(2,1)S(1)}, u32[]{:S(2)}, u32[]{:S(2)}) collective-permute-start(bf16[4,256,256]{2,1,0:T(8,128)(2,1)S(1)} %hidden_grad.8), channel_id=1, source_target_pairs={{0,16},{1,5},{2,18},{3,7},{4,20},{5,1},{6,22},{7,3},{8,24},{9,13},... | collective-permute-start | bytes 1572872 | tf_op jit(solution)/shard_map/hidden_grad/ppermute | solution.py:34
  94.4 11.2 %collective-permute-start.38 = (bf16[4,256,256]{2,1,0:T(8,128)(2,1)S(1)}, bf16[4,256,256]{2,1,0:T(8,128)(2,1)S(1)}, u32[]{:S(2)}, u32[]{:S(2)}) collective-permute-start(bf16[4,256,256]{2,1,0:T(8,128)(2,1)S(1)} %hidden_grad.9), channel_id=1, source_target_pairs={{0,24},{1,7},{2,26},{3,1},{4,28},{5,3},{6,30},{7,5},{8,0},{9,15},{... | collective-permute-start | bytes 1572872 | tf_op jit(solution)/shard_map/hidden_grad/ppermute | solution.py:34
  106.0 6.8 %collective-permute-start.40 = (bf16[256,256]{1,0:T(8,128)(2,1)S(1)}, bf16[256,256]{1,0:T(8,128)(2,1)S(1)}, u32[]{:S(2)}, u32[]{:S(2)}) collective-permute-start(bf16[256,256]{1,0:T(8,128)(2,1)S(1)} %get-tuple-element.124), channel_id=1, source_target_pairs={{0,4},{1,17},{2,6},{3,19},{4,0},{5,21},{6,2},{7,23},{8,12},{9,25},... | collective-permute-start | bytes 393224 | tf_op jit(solution)/shard_map/reduce_second/ppermute | solution.py:34
  113.9 6.1 %collective-permute-start.43 = (bf16[64,256]{1,0:T(8,128)(2,1)S(1)}, bf16[64,256]{1,0:T(8,128)(2,1)S(1)}, u32[]{:S(2)}, u32[]{:S(2)}) collective-permute-start(bf16[64,256]{1,0:T(8,128)(2,1)S(1)} %get-tuple-element.127), channel_id=1, source_target_pairs={{0,160},{1,33},{2,162},{3,35},{4,164},{5,37},{6,166},{7,39},{8,168... | collective-permute-start | bytes 98312 | tf_op jit(solution)/shard_map/reduce_tok/ppermute | solution.py:34
  114.9 6.8 %collective-permute-start.44 = (bf16[64,256]{1,0:T(8,128)(2,1)S(1)}, bf16[64,256]{1,0:T(8,128)(2,1)S(1)}, u32[]{:S(2)}, u32[]{:S(2)}) collective-permute-start(bf16[64,256]{1,0:T(8,128)(2,1)S(1)} %get-tuple-element.128), channel_id=1, source_target_pairs={{0,192},{1,65},{2,194},{3,67},{4,196},{5,69},{6,198},{7,71},{8,200... | collective-permute-start | bytes 98312 | tf_op jit(solution)/shard_map/reduce_tok/ppermute | solution.py:34
  122.9 5.2 %collective-permute-start.46 = (bf16[64,128]{1,0:T(8,128)(2,1)S(1)}, bf16[64,128]{1,0:T(8,128)(2,1)S(1)}, u32[]{:S(2)}, u32[]{:S(2)}) collective-permute-start(bf16[64,128]{1,0:T(8,128)(2,1)S(1)} %get-tuple-element.131), channel_id=1, source_target_pairs={{0,1},{1,0},{2,3},{3,2},{4,5},{5,4},{6,7},{7,6},{8,9},{9,8},{10,11... | collective-permute-start | bytes 49160 | tf_op jit(solution)/shard_map/hidden_out/ppermute | solution.py:30
  (27 other events, 144.3 us)

commit v2 on v1

--- a/solution.py
+++ b/solution.py
@@ -491,19 +491,21 @@
 
     with jax.named_scope("gather_tok"):
         blocks = [states] + [send(states, t=d) for d in (1, 2, 3)]
+    with jax.named_scope("gather_tok"):
+        place, *blocks = lax.optimization_barrier((place, *blocks))
+        block = jnp.stack(blocks)
+    with jax.named_scope("gather_first"):
+        blocks = [block] + [send_by_core(block, {"x": d}, {"y": d}) for d in (1, 2, 3)]
     with jax.named_scope("stage"):
         head_t, *halves = stage(place, head[0].T)
         head_t, *blocks = lax.optimization_barrier((head_t, *blocks))
-        halves = [send(half, c=1) for half in halves]
-    with jax.named_scope("gather_tok"):
-        block = jnp.stack(blocks)
-    with jax.named_scope("gather_first"):
-        blocks = [block] + [send_by_core(block, {"x": d}, {"y": d}) for d in (1, 2, 3)]
     with jax.named_scope("gather_first"):
         block = jnp.stack(blocks)
     with jax.named_scope("gather_second"):
         own = [block] + [send_by_core(block, {"y": d}, {"x": d}) for d in (1, 2, 3)]
     own[1], halves = lax.optimization_barrier((own[1], halves))
+    with jax.named_scope("stage"):
+        halves = [send(half, c=1) for half in halves]
     with jax.named_scope("gather_cores"):
         other = [send(block, c=1) for block in own[:3]]
         own[3], *other = lax.optimization_barrier((own[3], *other))
@@ -512,6 +514,7 @@
         sent = send_both_ways(first_half(place, own))
     with jax.named_scope("own_logits"):
         hidden_own, part = own_logits(place, head_t, own)
+        part, halves = lax.optimization_barrier((part, halves))
     with jax.named_scope("logits"):
         hidden_other, scaled, short, local = logits_parts(place, head_t, other, part)
 

time: 131 us -> 131 us (level)
    ppermute x18, starting transfers between devices: 31.3 us -> 23.9 us  [send_by_core(): lax.ppermute(block, AXES, route(lambda place: odd if place['c'] else even))]
    ppermute x28, starting transfers between devices: 39.7 us -> 46.7 us  [send(): return lax.ppermute(block, AXES, route(lambda place: shift))]
    ppermute x18, waiting for transfers between devices: 18.7 us -> 20 us  [send_by_core(): lax.ppermute(block, AXES, route(lambda place: odd if place['c'] else even))]
    unnamed x8 -> x6, local copies, waits for them, and re-layouts: 3.36 us -> 3.36 us
  transfers between devices with their start and end apart: 47 -> 47, of which waited for: 24 -> 22; matrix products, arithmetic and copies ran while one was open for 0% -> 0% of each run, Pallas kernels for 14% -> 14%
where the time goes in v2:
time: 131 us
  starting transfers between devices  71.6 us (55%)
  waiting for transfers between devices  31.4 us (24%)
  Pallas kernels  22.4 us (17%)
  local copies, waits for them, and re-layouts  3.44 us (3%)
    ppermute x28, starting transfers between devices, send(): return lax.ppermute(block, AXES, route(lambda place: shift))  46.7 us
    ppermute x18, starting transfers between devices, send_by_core(): lax.ppermute(block, AXES, route(lambda place: odd if place['c'] else even))  23.9 us
    ppermute x18, waiting for transfers between devices, send_by_core(): lax.ppermute(block, AXES, route(lambda place: odd if place['c'] else even))  20 us
    ppermute x28, waiting for transfers between devices, send(): return lax.ppermute(block, AXES, route(lambda place: shift))  11.4 us
    pallas_call x4, Pallas kernels, products(): pl.pallas_call(functools.partial(products_kernel, d), out_shape=jax.Shape...  4.8 us
    pallas_call x1, Pallas kernels, head_grad_half(): pl.pallas_call(head_grad_kernel, grid_spec=pltpu.PrefetchScalarGridSpec(n...  4.37 us
    unnamed x6, local copies, waits for them, and re-layouts  3.36 us
    pallas_call x1, Pallas kernels, logits_parts(): pl.pallas_call(logits_kernel, out_shape=[jax.ShapeDtypeStruct((4, toks, 4...  3.14 us
  transfers between devices with their start and end apart: 47, of which 22 were waited for; matrix products, arithmetic and copies ran while one was open for 0% of the time, Pallas kernels for 14%

profile of v2, /device:TPU:1, one launch (start us, length us, event | category | flops | bytes accessed | tf_op | source)
XLA Modules:
  0.0 130.5 jit_solution(12063475846071141956)
XLA Ops:
  0.6 6.9 %collective-permute-start.2 = (bf16[64,256]{1,0:T(8,128)(2,1)}, bf16[64,256]{1,0:T(8,128)(2,1)S(1)}, u32[]{:S(2)}, u32[]{:S(2)}) collective-permute-start(bf16[64,256]{1,0:T(8,128)(2,1)} %bitcast.28), channel_id=1, source_target_pairs={{0,96},{1,97},{2,98},{3,99},{4,100},{5,101},{6,102},{7,103},{8,104... | collective-permute-start | bytes 98312 | tf_op jit(solution)/shard_map/gather_tok/ppermute | solution.py:30
  8.5 2.3 %collective-permute-start = (bf16[64,256]{1,0:T(8,128)(2,1)}, bf16[64,256]{1,0:T(8,128)(2,1)S(1)}, u32[]{:S(2)}, u32[]{:S(2)}) collective-permute-start(bf16[64,256]{1,0:T(8,128)(2,1)} %bitcast.30), channel_id=1, source_target_pairs={{0,32},{1,33},{2,34},{3,35},{4,36},{5,37},{6,38},{7,39},{8,40},{9,... | collective-permute-start | bytes 98312 | tf_op jit(solution)/shard_map/gather_tok/ppermute | solution.py:30
  10.9 3.5 %collective-permute-done.1 = bf16[64,256]{1,0:T(8,128)(2,1)S(1)} collective-permute-done((bf16[64,256]{1,0:T(8,128)(2,1)}, bf16[64,256]{1,0:T(8,128)(2,1)S(1)}, u32[]{:S(2)}, u32[]{:S(2)}) %collective-permute-start.1) | collective-permute-done | bytes 32800 | tf_op jit(solution)/shard_map/gather_tok/ppermute | solution.py:30
  15.2 2.8 %collective-permute-start.5 = (bf16[4,64,256]{2,1,0:T(8,128)(2,1)S(1)}, bf16[4,64,256]{2,1,0:T(8,128)(2,1)S(1)}, u32[]{:S(2)}, u32[]{:S(2)}) collective-permute-start(bf16[4,64,256]{2,1,0:T(8,128)(2,1)S(1)} %pad_maximum_fusion.1), channel_id=1, source_target_pairs={{0,24},{1,7},{2,26},{3,1},{4,28},{5,3},{6,30},{7,5},{8,0},{9,15},{... | collective-permute-start | bytes 393224 | tf_op jit(solution)/shard_map/gather_first/ppermute | solution.py:34
  19.1 3.3 %copy-done = bf16[1,8192,501]{1,2,0:T(8,128)(2,1)S(1)} copy-done((bf16[1,8192,501]{1,2,0:T(8,128)(2,1)S(1)}, bf16[1,8192,501]{1,2,0:T(8,128)(2,1)}, u32[]{:S(2)}) %copy-start) | copy-done | bytes 8208408
  22.4 1.9 %stage.1 = (bf16[501,8192]{1,0:T(8,128)(2,1)S(1)}, bf16[501,512]{1,0:T(8,128)(2,1)S(1)}, bf16[501,512]{1,0:T(8,128)(2,1)S(1)}, bf16[501,512]{1,0:T(8,128)(2,1)S(...) custom-call(s32[5]{0:T(128)S(1)} %stack.53.place_ref, ...), custom_call_target="tpu_custom_call" | custom-call | tf_op jit(solution)/shard_map/stage/pallas_call | solution.py:72
  25.1 2.5 %collective-permute-start.10 = (bf16[4,4,64,256]{3,2,1,0:T(8,128)(2,1)S(1)}, bf16[4,4,64,256]{3,2,1,0:T(8,128)(2,1)S(1)}, u32[]{:S(2)}, u32[]{:S(2)}) collective-permute-start(bf16[4,4,64,256]{3,2,1,0:T(8,128)(2,1)S(1)} %pad_maximum_fusion.refs_0_), channel_id=1, source_target_pairs={{0,4},{1,17},{2,6},{3,19},{4,0},{5,21},{6,2},{7,23},{8,12},{9,25},... | collective-permute-start | bytes 1572872 | tf_op jit(solution)/shard_map/gather_second/ppermute | solution.py:34
  28.0 4.2 %collective-permute-start.7 = (bf16[4,4,64,256]{3,2,1,0:T(8,128)(2,1)S(1)}, bf16[4,4,64,256]{3,2,1,0:T(8,128)(2,1)S(1)}, u32[]{:S(2)}, u32[]{:S(2)}) collective-permute-start(bf16[4,4,64,256]{3,2,1,0:T(8,128)(2,1)S(1)} %pad_maximum_fusion.refs_0_), channel_id=1, source_target_pairs={{0,1},{1,0},{2,3},{3,2},{4,5},{5,4},{6,7},{7,6},{8,9},{9,8},{10,11... | collective-permute-start | bytes 1572872 | tf_op jit(solution)/shard_map/gather_cores/ppermute | solution.py:30
  35.1 4.0 %collective-permute-start.11 = (bf16[4,4,64,256]{3,2,1,0:T(8,128)(2,1)S(1)}, bf16[4,4,64,256]{3,2,1,0:T(8,128)(2,1)S(1)}, u32[]{:S(2)}, u32[]{:S(2)}) collective-permute-start(bf16[4,4,64,256]{3,2,1,0:T(8,128)(2,1)S(1)} %collective-permute-done.10.refs_2_), channel_id=1, source_target_pairs={{0,1},{1,0},{2,3},{3,2},{4,5},{5,4},{6,7},{7,6},{8,9},{9,8},{10,11... | collective-permute-start | bytes 1572872 | tf_op jit(solution)/shard_map/gather_cores/ppermute | solution.py:30
  40.7 4.0 %collective-permute-start.9 = (bf16[4,4,64,256]{3,2,1,0:T(8,128)(2,1)S(1)}, bf16[4,4,64,256]{3,2,1,0:T(8,128)(2,1)S(1)}, u32[]{:S(2)}, u32[]{:S(2)}) collective-permute-start(bf16[4,4,64,256]{3,2,1,0:T(8,128)(2,1)S(1)} %collective-permute-done.8.refs_1_), channel_id=1, source_target_pairs={{0,1},{1,0},{2,3},{3,2},{4,5},{5,4},{6,7},{7,6},{8,9},{9,8},{10,11... | collective-permute-start | bytes 1572872 | tf_op jit(solution)/shard_map/gather_cores/ppermute | solution.py:30
  50.2 2.9 %own_logits.1 = (bf16[4,256,1024]{2,1,0:T(8,128)(2,1)S(1)}, f32[501,256]{1,0:T(8,128)S(1)}) custom-call(s32[5]{0:T(128)S(1)} %stack.53.place_ref, bf16[501,8192]{1,0:T(8,128)(2,1)S(1)} %get-tuple-element.87.head_ref, bf16[4,4,64,256]{3,2,1,0:T(8,128)(2,1)S(1)} %pad_maximum_fusion.refs_0_, bf16[4,4,64,256]{3,2,1,0:T(8,128)(2,1)S(1)} %collective-permute-done.8.refs_1_, ...), custom_call_target="tpu_custom_call" | custom-call | tf_op jit(solution)/shard_map/own_logits/pallas_call | solution.py:162
  53.2 3.1 %logits.1 = (bf16[4,256,1024]{2,1,0:T(8,128)(2,1)S(1)}, f32[501,256]{1,0:T(8,128)S(1)}, bf16[501,256]{1,0:T(8,128)(2,1)S(1)}, f32[8,256]{1,0:T(8,128)S(1)}) custom-call(s32[5]{0:T(128)S(1)} %stack.53.place_ref, bf16[501,8192]{1,0:T(8,128)(2,1)S(1)} %get-tuple-element.87.head_ref, bf16[4,4,64,256]{3,2,1,0:T(8,128)(2,1)S(1)} %collective-permute-done.7.refs_0_, ...), custom_call_target="tpu_custom_call" | custom-call | tf_op jit(solution)/shard_map/logits/pallas_call | solution.py:195
  60.5 2.2 %collective-permute-start.25 = (f32[8,256]{1,0:T(8,128)S(1)}, f32[8,256]{1,0:T(8,128)S(1)}, u32[]{:S(2)}, u32[]{:S(2)}) collective-permute-start(f32[8,256]{1,0:T(8,128)S(1)} %collective-permute-done.24.refs_2_), channel_id=1, source_target_pairs={{0,1},{1,0},{2,3},{3,2},{4,5},{5,4},{6,7},{7,6},{8,9},{9,8},{10,11... | collective-permute-start | bytes 24584 | tf_op jit(solution)/shard_map/stats/ppermute | solution.py:30
  65.6 2.4 %collective-permute-start.27 = (f32[8,256]{1,0:T(8,128)S(1)}, f32[8,256]{1,0:T(8,128)S(1)}, u32[]{:S(2)}, u32[]{:S(2)}) collective-permute-start(f32[8,256]{1,0:T(8,128)S(1)} %stats.5.refs_0_), channel_id=1, source_target_pairs={{0,4},{1,5},{2,6},{3,7},{4,0},{5,1},{6,2},{7,3},{8,12},{9,13},{10,... | collective-permute-start | bytes 24584 | tf_op jit(solution)/shard_map/stats/ppermute | solution.py:30
  67.9 2.1 %collective-permute-start.29 = (f32[8,256]{1,0:T(8,128)S(1)}, f32[8,256]{1,0:T(8,128)S(1)}, u32[]{:S(2)}, u32[]{:S(2)}) collective-permute-start(f32[8,256]{1,0:T(8,128)S(1)} %collective-permute-done.28.refs_2_), channel_id=1, source_target_pairs={{0,1},{1,0},{2,3},{3,2},{4,5},{5,4},{6,7},{7,6},{8,9},{9,8},{10,11... | collective-permute-start | bytes 24584 | tf_op jit(solution)/shard_map/stats/ppermute | solution.py:30
  72.7 3.7 %collective-permute-start.30 = (f32[8,256]{1,0:T(8,128)S(1)}, f32[8,256]{1,0:T(8,128)S(1)}, u32[]{:S(2)}, u32[]{:S(2)}) collective-permute-start(f32[8,256]{1,0:T(8,128)S(1)} %stats.6.refs_0_), channel_id=1, source_target_pairs={{0,64},{1,65},{2,66},{3,67},{4,68},{5,69},{6,70},{7,71},{8,72},{9,... | collective-permute-start | bytes 24584 | tf_op jit(solution)/shard_map/stats/ppermute | solution.py:30
  82.6 4.5 %collective-permute-start.35 = (bf16[256,501]{1,0:T(8,128)(2,1)S(1)}, bf16[256,501]{1,0:T(8,128)(2,1)S(1)}, u32[]{:S(2)}, u32[]{:S(2)}) collective-permute-start(bf16[256,501]{1,0:T(8,128)(2,1)S(1)} %get-tuple-element.143.turned_ref), channel_id=1, source_target_pairs={{0,1},{1,0},{2,3},{3,2},{4,5},{5,4},{6,7},{7,6},{8,9},{9,8},{10,11... | collective-permute-start | bytes 769544 | tf_op jit(solution)/shard_map/hidden_grad/ppermute | solution.py:30
  90.8 2.2 %collective-permute-start.36 = (bf16[4,256,256]{2,1,0:T(8,128)(2,1)S(1)}, bf16[4,256,256]{2,1,0:T(8,128)(2,1)S(1)}, u32[]{:S(2)}, u32[]{:S(2)}) collective-permute-start(bf16[4,256,256]{2,1,0:T(8,128)(2,1)S(1)} %hidden_grad.8), channel_id=1, source_target_pairs={{0,16},{1,5},{2,18},{3,7},{4,20},{5,1},{6,22},{7,3},{8,24},{9,13},... | collective-permute-start | bytes 1572872 | tf_op jit(solution)/shard_map/hidden_grad/ppermute | solution.py:34
  95.1 9.3 %collective-permute-done.37.refs_1_ = bf16[4,256,256]{2,1,0:T(8,128)(2,1)S(1)} collective-permute-done((bf16[4,256,256]{2,1,0:T(8,128)(2,1)S(1)}, bf16[4,256,256]{2,1,0:T(8,128)(2,1)S(1)}, u32[]{:S(2)}, u32[]{:S(2)}) %collective-permute-start.37) | collective-permute-done | bytes 524320 | tf_op jit(solution)/shard_map/hidden_grad/ppermute | solution.py:34
  104.4 4.4 %hidden_grad.10 = bf16[501,4096]{1,0:T(8,128)(2,1)} custom-call(s32[5]{0:T(128)S(1)} %stack.53.place_ref, bf16[501,256]{1,0:T(8,128)(2,1)S(1)} %get-tuple-element.138.grad_ref, bf16[4,256,1024]{2,1,0:T(8,128)(2,1)S(1)} %get-tuple-element.139.own_ref, bf16[4,256,1024]{2,1,0:T(8,128)(2,1)S(1)} %get-tuple-element.140.other_ref, ...), custom_call_target="tpu_custom_call" | custom-call | tf_op jit(solution)/shard_map/hidden_grad/pallas_call | solution.py:461
  110.4 3.2 %collective-permute-start.40 = (bf16[256,256]{1,0:T(8,128)(2,1)S(1)}, bf16[256,256]{1,0:T(8,128)(2,1)S(1)}, u32[]{:S(2)}, u32[]{:S(2)}) collective-permute-start(bf16[256,256]{1,0:T(8,128)(2,1)S(1)} %get-tuple-element.152), channel_id=1, source_target_pairs={{0,4},{1,17},{2,6},{3,19},{4,0},{5,21},{6,2},{7,23},{8,12},{9,25},... | collective-permute-start | bytes 393224 | tf_op jit(solution)/shard_map/reduce_second/ppermute | solution.py:34
  115.5 1.9 %collective-permute-done.40.refs_2_ = bf16[256,256]{1,0:T(8,128)(2,1)S(1)} collective-permute-done((bf16[256,256]{1,0:T(8,128)(2,1)S(1)}, bf16[256,256]{1,0:T(8,128)(2,1)S(1)}, u32[]{:S(2)}, u32[]{:S(2)}) %collective-permute-start.40) | collective-permute-done | bytes 131104 | tf_op jit(solution)/shard_map/reduce_second/ppermute | solution.py:34
  118.1 1.9 %collective-permute-start.43 = (bf16[64,256]{1,0:T(8,128)(2,1)S(1)}, bf16[64,256]{1,0:T(8,128)(2,1)S(1)}, u32[]{:S(2)}, u32[]{:S(2)}) collective-permute-start(bf16[64,256]{1,0:T(8,128)(2,1)S(1)} %get-tuple-element.155), channel_id=1, source_target_pairs={{0,160},{1,33},{2,162},{3,35},{4,164},{5,37},{6,166},{7,39},{8,168... | collective-permute-start | bytes 98312 | tf_op jit(solution)/shard_map/reduce_tok/ppermute | solution.py:34
  124.5 2.6 %collective-permute-done.44.refs_2_ = bf16[64,256]{1,0:T(8,128)(2,1)S(1)} collective-permute-done((bf16[64,256]{1,0:T(8,128)(2,1)S(1)}, bf16[64,256]{1,0:T(8,128)(2,1)S(1)}, u32[]{:S(2)}, u32[]{:S(2)}) %collective-permute-start.44) | collective-permute-done | bytes 32800 | tf_op jit(solution)/shard_map/reduce_tok/ppermute | solution.py:34
  (98 shorter events, 47.8 us)
Async XLA Ops:
  0.6 10.3 %collective-permute-start.2 = (bf16[64,256]{1,0:T(8,128)(2,1)}, bf16[64,256]{1,0:T(8,128)(2,1)S(1)}, u32[]{:S(2)}, u32[]{:S(2)}) collective-permute-start(bf16[64,256]{1,0:T(8,128)(2,1)} %bitcast.28), channel_id=1, source_target_pairs={{0,96},{1,97},{2,98},{3,99},{4,100},{5,101},{6,102},{7,103},{8,104... | collective-permute-start | bytes 98312 | tf_op jit(solution)/shard_map/gather_tok/ppermute | solution.py:30
  7.6 6.9 %collective-permute-start.1 = (bf16[64,256]{1,0:T(8,128)(2,1)}, bf16[64,256]{1,0:T(8,128)(2,1)S(1)}, u32[]{:S(2)}, u32[]{:S(2)}) collective-permute-start(bf16[64,256]{1,0:T(8,128)(2,1)} %bitcast.29), channel_id=1, source_target_pairs={{0,64},{1,65},{2,66},{3,67},{4,68},{5,69},{6,70},{7,71},{8,72},{9,... | collective-permute-start | bytes 98312 | tf_op jit(solution)/shard_map/gather_tok/ppermute | solution.py:30
  8.5 5.9 %collective-permute-start = (bf16[64,256]{1,0:T(8,128)(2,1)}, bf16[64,256]{1,0:T(8,128)(2,1)S(1)}, u32[]{:S(2)}, u32[]{:S(2)}) collective-permute-start(bf16[64,256]{1,0:T(8,128)(2,1)} %bitcast.30), channel_id=1, source_target_pairs={{0,32},{1,33},{2,34},{3,35},{4,36},{5,37},{6,38},{7,39},{8,40},{9,... | collective-permute-start | bytes 98312 | tf_op jit(solution)/shard_map/gather_tok/ppermute | solution.py:30
  15.2 9.1 %collective-permute-start.5 = (bf16[4,64,256]{2,1,0:T(8,128)(2,1)S(1)}, bf16[4,64,256]{2,1,0:T(8,128)(2,1)S(1)}, u32[]{:S(2)}, u32[]{:S(2)}) collective-permute-start(bf16[4,64,256]{2,1,0:T(8,128)(2,1)S(1)} %pad_maximum_fusion.1), channel_id=1, source_target_pairs={{0,24},{1,7},{2,26},{3,1},{4,28},{5,3},{6,30},{7,5},{8,0},{9,15},{... | collective-permute-start | bytes 393224 | tf_op jit(solution)/shard_map/gather_first/ppermute | solution.py:34
  18.0 6.3 %collective-permute-start.4 = (bf16[4,64,256]{2,1,0:T(8,128)(2,1)S(1)}, bf16[4,64,256]{2,1,0:T(8,128)(2,1)S(1)}, u32[]{:S(2)}, u32[]{:S(2)}) collective-permute-start(bf16[4,64,256]{2,1,0:T(8,128)(2,1)S(1)} %pad_maximum_fusion.1), channel_id=1, source_target_pairs={{0,16},{1,5},{2,18},{3,7},{4,20},{5,1},{6,22},{7,3},{8,24},{9,13},... | collective-permute-start | bytes 393224 | tf_op jit(solution)/shard_map/gather_first/ppermute | solution.py:34
  18.4 6.7 %collective-permute-start.3 = (bf16[4,64,256]{2,1,0:T(8,128)(2,1)S(1)}, bf16[4,64,256]{2,1,0:T(8,128)(2,1)S(1)}, u32[]{:S(2)}, u32[]{:S(2)}) collective-permute-start(bf16[4,64,256]{2,1,0:T(8,128)(2,1)S(1)} %pad_maximum_fusion.1), channel_id=1, source_target_pairs={{0,8},{1,3},{2,10},{3,5},{4,12},{5,7},{6,14},{7,1},{8,16},{9,11},{... | collective-permute-start | bytes 393224 | tf_op jit(solution)/shard_map/gather_first/ppermute | solution.py:34
  25.1 10.0 %collective-permute-start.10 = (bf16[4,4,64,256]{3,2,1,0:T(8,128)(2,1)S(1)}, bf16[4,4,64,256]{3,2,1,0:T(8,128)(2,1)S(1)}, u32[]{:S(2)}, u32[]{:S(2)}) collective-permute-start(bf16[4,4,64,256]{3,2,1,0:T(8,128)(2,1)S(1)} %pad_maximum_fusion.refs_0_), channel_id=1, source_target_pairs={{0,4},{1,17},{2,6},{3,19},{4,0},{5,21},{6,2},{7,23},{8,12},{9,25},... | collective-permute-start | bytes 1572872 | tf_op jit(solution)/shard_map/gather_second/ppermute | solution.py:34
  27.7 13.0 %collective-permute-start.8 = (bf16[4,4,64,256]{3,2,1,0:T(8,128)(2,1)S(1)}, bf16[4,4,64,256]{3,2,1,0:T(8,128)(2,1)S(1)}, u32[]{:S(2)}, u32[]{:S(2)}) collective-permute-start(bf16[4,4,64,256]{3,2,1,0:T(8,128)(2,1)S(1)} %pad_maximum_fusion.refs_0_), channel_id=1, source_target_pairs={{0,2},{1,9},{2,4},{3,11},{4,6},{5,13},{6,0},{7,15},{8,10},{9,17},{... | collective-permute-start | bytes 1572872 | tf_op jit(solution)/shard_map/gather_second/ppermute | solution.py:34
  28.0 16.7 %collective-permute-start.7 = (bf16[4,4,64,256]{3,2,1,0:T(8,128)(2,1)S(1)}, bf16[4,4,64,256]{3,2,1,0:T(8,128)(2,1)S(1)}, u32[]{:S(2)}, u32[]{:S(2)}) collective-permute-start(bf16[4,4,64,256]{3,2,1,0:T(8,128)(2,1)S(1)} %pad_maximum_fusion.refs_0_), channel_id=1, source_target_pairs={{0,1},{1,0},{2,3},{3,2},{4,5},{5,4},{6,7},{7,6},{8,9},{9,8},{10,11... | collective-permute-start | bytes 1572872 | tf_op jit(solution)/shard_map/gather_cores/ppermute | solution.py:30
  32.2 12.9 %collective-permute-start.6 = (bf16[4,4,64,256]{3,2,1,0:T(8,128)(2,1)S(1)}, bf16[4,4,64,256]{3,2,1,0:T(8,128)(2,1)S(1)}, u32[]{:S(2)}, u32[]{:S(2)}) collective-permute-start(bf16[4,4,64,256]{3,2,1,0:T(8,128)(2,1)S(1)} %pad_maximum_fusion.refs_0_), channel_id=1, source_target_pairs={{0,6},{1,25},{2,0},{3,27},{4,2},{5,29},{6,4},{7,31},{8,14},{9,1},{... | collective-permute-start | bytes 1572872 | tf_op jit(solution)/shard_map/gather_second/ppermute | solution.py:34
  35.1 10.2 %collective-permute-start.11 = (bf16[4,4,64,256]{3,2,1,0:T(8,128)(2,1)S(1)}, bf16[4,4,64,256]{3,2,1,0:T(8,128)(2,1)S(1)}, u32[]{:S(2)}, u32[]{:S(2)}) collective-permute-start(bf16[4,4,64,256]{3,2,1,0:T(8,128)(2,1)S(1)} %collective-permute-done.10.refs_2_), channel_id=1, source_target_pairs={{0,1},{1,0},{2,3},{3,2},{4,5},{5,4},{6,7},{7,6},{8,9},{9,8},{10,11... | collective-permute-start | bytes 1572872 | tf_op jit(solution)/shard_map/gather_cores/ppermute | solution.py:30
  40.7 5.5 %collective-permute-start.9 = (bf16[4,4,64,256]{3,2,1,0:T(8,128)(2,1)S(1)}, bf16[4,4,64,256]{3,2,1,0:T(8,128)(2,1)S(1)}, u32[]{:S(2)}, u32[]{:S(2)}) collective-permute-start(bf16[4,4,64,256]{3,2,1,0:T(8,128)(2,1)S(1)} %collective-permute-done.8.refs_1_), channel_id=1, source_target_pairs={{0,1},{1,0},{2,3},{3,2},{4,5},{5,4},{6,7},{7,6},{8,9},{9,8},{10,11... | collective-permute-start | bytes 1572872 | tf_op jit(solution)/shard_map/gather_cores/ppermute | solution.py:30
  47.3 16.2 %collective-permute-start.26 = (bf16[2,256,1024]{2,1,0:T(8,128)(2,1)S(1)}, bf16[2,256,1024]{2,1,0:T(8,128)(2,1)S(1)}, u32[]{:S(2)}, u32[]{:S(2)}) collective-permute-start(bf16[2,256,1024]{2,1,0:T(8,128)(2,1)S(1)} %student_hidden.1), channel_id=1, source_target_pairs={{0,128},{1,225},{2,130},{3,227},{4,132},{5,229},{6,134},{7,231},{8... | collective-permute-start | bytes 3145736 | tf_op jit(solution)/shard_map/student_hidden/ppermute | solution.py:41
  63.6 19.0 %collective-permute-start.34 = (bf16[2,256,1024]{2,1,0:T(8,128)(2,1)S(1)}, bf16[2,256,1024]{2,1,0:T(8,128)(2,1)S(1)}, u32[]{:S(2)}, u32[]{:S(2)}) collective-permute-start(bf16[2,256,1024]{2,1,0:T(8,128)(2,1)S(1)} %collective-permute-done.26.sent_ref), channel_id=1, source_target_pairs={{0,1},{1,0},{2,3},{3,2},{4,5},{5,4},{6,7},{7,6},{8,9},{9,8},{10,11... | collective-permute-start | bytes 3145736 | tf_op jit(solution)/shard_map/student_hidden/ppermute | solution.py:30
  64.0 16.3 %collective-permute-start.22 = (bf16[501,256]{1,0:T(8,128)(2,1)S(1)}, bf16[501,256]{1,0:T(8,128)(2,1)S(1)}, u32[]{:S(2)}, u32[]{:S(2)}) collective-permute-start(bf16[501,256]{1,0:T(8,128)(2,1)S(1)} %get-tuple-element.118), channel_id=1, source_target_pairs={{0,128},{1,129},{2,130},{3,131},{4,132},{5,133},{6,134},{7,135},{8... | collective-permute-start | bytes 769544 | tf_op jit(solution)/shard_map/exchange_scaled/ppermute | solution.py:30
  70.8 5.6 %collective-permute-start.31 = (f32[8,256]{1,0:T(8,128)S(1)}, f32[8,256]{1,0:T(8,128)S(1)}, u32[]{:S(2)}, u32[]{:S(2)}) collective-permute-start(f32[8,256]{1,0:T(8,128)S(1)} %stats.6.refs_0_), channel_id=1, source_target_pairs={{0,32},{1,97},{2,34},{3,99},{4,36},{5,101},{6,38},{7,103},{8,40},{... | collective-permute-start | bytes 24584 | tf_op jit(solution)/shard_map/stats/ppermute | solution.py:34
  72.7 6.4 %collective-permute-start.30 = (f32[8,256]{1,0:T(8,128)S(1)}, f32[8,256]{1,0:T(8,128)S(1)}, u32[]{:S(2)}, u32[]{:S(2)}) collective-permute-start(f32[8,256]{1,0:T(8,128)S(1)} %stats.6.refs_0_), channel_id=1, source_target_pairs={{0,64},{1,65},{2,66},{3,67},{4,68},{5,69},{6,70},{7,71},{8,72},{9,... | collective-permute-start | bytes 24584 | tf_op jit(solution)/shard_map/stats/ppermute | solution.py:30
  82.6 5.6 %collective-permute-start.35 = (bf16[256,501]{1,0:T(8,128)(2,1)S(1)}, bf16[256,501]{1,0:T(8,128)(2,1)S(1)}, u32[]{:S(2)}, u32[]{:S(2)}) collective-permute-start(bf16[256,501]{1,0:T(8,128)(2,1)S(1)} %get-tuple-element.143.turned_ref), channel_id=1, source_target_pairs={{0,1},{1,0},{2,3},{3,2},{4,5},{5,4},{6,7},{7,6},{8,9},{9,8},{10,11... | collective-permute-start | bytes 769544 | tf_op jit(solution)/shard_map/hidden_grad/ppermute | solution.py:30
  89.2 15.2 %collective-permute-start.37 = (bf16[4,256,256]{2,1,0:T(8,128)(2,1)S(1)}, bf16[4,256,256]{2,1,0:T(8,128)(2,1)S(1)}, u32[]{:S(2)}, u32[]{:S(2)}) collective-permute-start(bf16[4,256,256]{2,1,0:T(8,128)(2,1)S(1)} %hidden_grad.7), channel_id=1, source_target_pairs={{0,8},{1,3},{2,10},{3,5},{4,12},{5,7},{6,14},{7,1},{8,16},{9,11},{... | collective-permute-start | bytes 1572872 | tf_op jit(solution)/shard_map/hidden_grad/ppermute | solution.py:34
  90.8 18.0 %collective-permute-start.36 = (bf16[4,256,256]{2,1,0:T(8,128)(2,1)S(1)}, bf16[4,256,256]{2,1,0:T(8,128)(2,1)S(1)}, u32[]{:S(2)}, u32[]{:S(2)}) collective-permute-start(bf16[4,256,256]{2,1,0:T(8,128)(2,1)S(1)} %hidden_grad.8), channel_id=1, source_target_pairs={{0,16},{1,5},{2,18},{3,7},{4,20},{5,1},{6,22},{7,3},{8,24},{9,13},... | collective-permute-start | bytes 1572872 | tf_op jit(solution)/shard_map/hidden_grad/ppermute | solution.py:34
  94.3 15.8 %collective-permute-start.38 = (bf16[4,256,256]{2,1,0:T(8,128)(2,1)S(1)}, bf16[4,256,256]{2,1,0:T(8,128)(2,1)S(1)}, u32[]{:S(2)}, u32[]{:S(2)}) collective-permute-start(bf16[4,256,256]{2,1,0:T(8,128)(2,1)S(1)} %hidden_grad.9), channel_id=1, source_target_pairs={{0,24},{1,7},{2,26},{3,1},{4,28},{5,3},{6,30},{7,5},{8,0},{9,15},{... | collective-permute-start | bytes 1572872 | tf_op jit(solution)/shard_map/hidden_grad/ppermute | solution.py:34
  110.4 6.9 %collective-permute-start.40 = (bf16[256,256]{1,0:T(8,128)(2,1)S(1)}, bf16[256,256]{1,0:T(8,128)(2,1)S(1)}, u32[]{:S(2)}, u32[]{:S(2)}) collective-permute-start(bf16[256,256]{1,0:T(8,128)(2,1)S(1)} %get-tuple-element.152), channel_id=1, source_target_pairs={{0,4},{1,17},{2,6},{3,19},{4,0},{5,21},{6,2},{7,23},{8,12},{9,25},... | collective-permute-start | bytes 393224 | tf_op jit(solution)/shard_map/reduce_second/ppermute | solution.py:34
  118.1 6.4 %collective-permute-start.43 = (bf16[64,256]{1,0:T(8,128)(2,1)S(1)}, bf16[64,256]{1,0:T(8,128)(2,1)S(1)}, u32[]{:S(2)}, u32[]{:S(2)}) collective-permute-start(bf16[64,256]{1,0:T(8,128)(2,1)S(1)} %get-tuple-element.155), channel_id=1, source_target_pairs={{0,160},{1,33},{2,162},{3,35},{4,164},{5,37},{6,166},{7,39},{8,168... | collective-permute-start | bytes 98312 | tf_op jit(solution)/shard_map/reduce_tok/ppermute | solution.py:34
  120.0 7.1 %collective-permute-start.44 = (bf16[64,256]{1,0:T(8,128)(2,1)S(1)}, bf16[64,256]{1,0:T(8,128)(2,1)S(1)}, u32[]{:S(2)}, u32[]{:S(2)}) collective-permute-start(bf16[64,256]{1,0:T(8,128)(2,1)S(1)} %get-tuple-element.156), channel_id=1, source_target_pairs={{0,192},{1,65},{2,194},{3,67},{4,196},{5,69},{6,198},{7,71},{8,200... | collective-permute-start | bytes 98312 | tf_op jit(solution)/shard_map/reduce_tok/ppermute | solution.py:34
  (26 other events, 141.7 us)
